TPU v7x, 512 devices: a whole 4x8x8 slice. The times are simulated.
512 devices in a mesh: ctx: 32 (over y, x), tp: 8 (over z_hi, core), dp: 2 (over z_lo).
Axes of the slice: x: 4, y: 8, z: 8 (z_hi: 4, z_lo: 2; z = z_hi * 2 + z_lo), core: 2. Of those that a mesh axis runs over, the one named last changes fastest.
Arguments:
- q_light: bfloat16 [8192, 4096], P(('dp', 'ctx'), 'tp'), parts along dimension 0, may hold values from -1.4 to 1.4
- k_light: bfloat16 [8192, 4096], P(('dp', 'ctx'), 'tp'), parts along dimension 0, may hold values from -1.35 to 1.35
- v_light: bfloat16 [8192, 4096], P(('dp', 'ctx'), 'tp'), parts along dimension 0, may hold values from -6.2 to 6.2
- g_light: bfloat16 [8192, 4096], P(('dp', 'ctx'), 'tp'), parts along dimension 0, may hold values from -6 to 6
- log_decay: float32 [8192, 32], P(('dp', 'ctx'), 'tp'), parts along dimension 0, may hold values from -0.6 to 0
- q_soft: bfloat16 [8192, 4096], P(('dp', 'ctx'), 'tp'), parts along dimension 0, may hold values from -125 to 125
- k_soft: bfloat16 [8192, 1024], P(('dp', 'ctx'), 'tp'), parts along dimension 0, may hold values from -5 to 5
- v_soft: bfloat16 [8192, 1024], P(('dp', 'ctx'), 'tp'), parts along dimension 0, may hold values from -6 to 6
- g_soft: bfloat16 [8192, 4096], P(('dp', 'ctx'), 'tp'), parts along dimension 0, may hold values from -6 to 6
Outputs:
- o_light: bfloat16 [8192, 4096], P(('dp', 'ctx'), 'tp'), parts along dimension 0
- dq_light: bfloat16 [8192, 4096], P(('dp', 'ctx'), 'tp'), parts along dimension 0
- dk_light: bfloat16 [8192, 4096], P(('dp', 'ctx'), 'tp'), parts along dimension 0
- dv_light: bfloat16 [8192, 4096], P(('dp', 'ctx'), 'tp'), parts along dimension 0
- o_soft: bfloat16 [8192, 4096], P(('dp', 'ctx'), 'tp'), parts along dimension 0
- dq_soft: bfloat16 [8192, 4096], P(('dp', 'ctx'), 'tp'), parts along dimension 0
- dk_soft: bfloat16 [8192, 1024], P(('dp', 'ctx'), 'tp'), parts along dimension 0
- dv_soft: bfloat16 [8192, 1024], P(('dp', 'ctx'), 'tp'), parts along dimension 0
There are 2 independent parts, one for each index of `dp`. A program takes and returns all parts, laid end to end along the dimension named above; each array names one. Nothing has to cross between parts.
All inputs are finite; a program needn't handle non-finite values.
Results may differ from a plain program's by a relative error of at most 0.015.
Values may be sent and summed in bfloat16 or wider, within the bound.
A program may use at most 128 MiB of HBM per device.

v0:
```python
import jax
import jax.numpy as jnp
from jax import lax
from jax.sharding import PartitionSpec as P

DH = 128


HIGHEST_PRECISION = lax.Precision.HIGHEST
MASKED_SCORE = -1e30


def prefix(value, axis, join, neutral, backward):
    count, mine = (lax.axis_size(axis), lax.axis_index(axis))
    pieces = jax.tree.map(lambda part: lax.all_gather(part, axis), value)
    if backward:
        pieces = jax.tree.map(lambda part: part[::-1], pieces)
        mine = count - 1 - mine
    so_far = jax.tree.map(
        lambda part, zero: jnp.full_like(part, 0) + jnp.asarray(zero, part.dtype), value, neutral
    )

    def turn(position, so_far):
        longer = join(so_far, jax.tree.map(lambda part: part[position], pieces))
        return jax.tree.map(lambda new, old: jnp.where(position < mine, new, old), longer, so_far)

    return lax.fori_loop(0, count - 1, turn, so_far)


def combine_states(earlier, later):
    return (earlier[0] * later[0], later[0][:, None, None] * earlier[1] + later[1])


def lightning(q_light, k_light, v_light, g_light, log_decay):
    row_count = q_light.shape[0]
    head_count = log_decay.shape[1]
    shaped = (row_count, head_count, DH)
    queries = q_light.reshape(shaped)
    key_rows = k_light.reshape(shaped)
    value_rows = v_light.reshape(shaped)
    out_grad = g_light.reshape(shaped)
    scaling = DH ** (-0.5)
    cumulative = jnp.cumsum(log_decay, axis=0)
    log_gaps = cumulative[:, None, :] - cumulative[None, :, :]
    causal = (jnp.arange(row_count)[:, None] >= jnp.arange(row_count)[None, :])[:, :, None]
    weights = jnp.where(causal, jnp.exp(jnp.where(causal, log_gaps, 0.0)), 0.0) * scaling
    weights = jnp.transpose(weights, (2, 0, 1))
    scores = jnp.einsum("thd,ihd->hti", queries, key_rows, preferred_element_type=jnp.float32)
    mixing = (scores * weights).astype(jnp.bfloat16)
    back_scores = jnp.einsum(
        "thd,ihd->hti", out_grad, value_rows, preferred_element_type=jnp.float32
    )
    back_mix = (back_scores * weights).astype(jnp.bfloat16)
    out_intra = jnp.einsum("hti,ihd->thd", mixing, value_rows, preferred_element_type=jnp.float32)
    value_intra = jnp.einsum("hti,thd->ihd", mixing, out_grad, preferred_element_type=jnp.float32)
    query_intra = jnp.einsum("hti,ihd->thd", back_mix, key_rows, preferred_element_type=jnp.float32)
    key_intra = jnp.einsum("hti,thd->ihd", back_mix, queries, preferred_element_type=jnp.float32)
    decay_in = jnp.exp(cumulative)
    decay_out = jnp.exp(cumulative[-1][None, :] - cumulative)
    block_decay = decay_in[-1]
    query_wide = queries.astype(jnp.float32)
    key_wide = key_rows.astype(jnp.float32)
    value_wide = value_rows.astype(jnp.float32)
    grad_wide = out_grad.astype(jnp.float32)
    state_local = jnp.einsum(
        "ih,ihd,ihe->hde", decay_out, key_wide, value_wide, precision=HIGHEST_PRECISION
    )
    grad_local = jnp.einsum(
        "th,thd,the->hde", decay_in, query_wide, grad_wide, precision=HIGHEST_PRECISION
    )
    identity = (jnp.ones((head_count,), jnp.float32), jnp.zeros((head_count, DH, DH), jnp.float32))
    prior_state = prefix((block_decay, state_local), "ctx", combine_states, identity, False)[1]
    later_grad = prefix((block_decay, grad_local), "ctx", combine_states, identity, True)[1]
    out_full = out_intra + scaling * decay_in[..., None] * jnp.einsum(
        "thd,hde->the", query_wide, prior_state, precision=HIGHEST_PRECISION
    )
    query_grad = query_intra + scaling * decay_in[..., None] * jnp.einsum(
        "the,hde->thd", grad_wide, prior_state, precision=HIGHEST_PRECISION
    )
    key_grad = key_intra + scaling * decay_out[..., None] * jnp.einsum(
        "ihe,hde->ihd", value_wide, later_grad, precision=HIGHEST_PRECISION
    )
    value_grad = value_intra + scaling * decay_out[..., None] * jnp.einsum(
        "ihd,hde->ihe", key_wide, later_grad, precision=HIGHEST_PRECISION
    )
    flat = (row_count, head_count * DH)
    return tuple(
        (
            item.reshape(flat).astype(jnp.bfloat16)
            for item in (out_full, query_grad, key_grad, value_grad)
        )
    )


def soft_scores(queries, key_piece, query_first, key_first):
    scores = jnp.einsum(
        "rkgd,pkd->kgrp", queries, key_piece, preferred_element_type=jnp.float32
    ) * DH ** (-0.5)
    query_pos = query_first + jnp.arange(queries.shape[0], dtype=jnp.int32)
    key_pos = key_first + jnp.arange(key_piece.shape[0], dtype=jnp.int32)
    allowed = query_pos[:, None] >= key_pos[None, :]
    return (scores, allowed)


def back_terms(
    queries, out_grad, key_piece, value_piece, query_first, key_first, log_totals, row_dots
):
    scores, allowed = soft_scores(queries, key_piece, query_first, key_first)
    soft_weights = jnp.where(allowed, jnp.exp(scores - log_totals[..., None]), 0.0)
    soft_rounded = soft_weights.astype(jnp.bfloat16)
    weight_grad = jnp.einsum(
        "rkgd,pkd->kgrp", out_grad, value_piece, preferred_element_type=jnp.float32
    )
    score_grad = (DH ** (-0.5) * soft_weights * (weight_grad - row_dots[..., None])).astype(
        jnp.bfloat16
    )
    return (soft_rounded, score_grad)


def shards(q_light, k_light, v_light, g_light, log_decay, q_soft, k_soft, v_soft, g_soft):
    o_light, dq_light, dk_light, dv_light = lightning(q_light, k_light, v_light, g_light, log_decay)
    row_count = q_soft.shape[0]
    kv_heads = k_soft.shape[1] // DH
    group_size = q_soft.shape[1] // k_soft.shape[1]
    queries = q_soft.reshape(row_count, kv_heads, group_size, DH)
    out_grad = g_soft.reshape(row_count, kv_heads, group_size, DH)
    own_keys = k_soft.reshape(row_count, kv_heads, DH)
    own_values = v_soft.reshape(row_count, kv_heads, DH)
    own_first = lax.axis_index("ctx") * row_count
    maxima = jnp.full((kv_heads, group_size, row_count), MASKED_SCORE, jnp.float32)
    key_piece = (lax.all_gather(k_soft, "ctx", axis=0, tiled=True),)[0].reshape(-1, kv_heads, DH)
    scores, allowed = soft_scores(queries, key_piece, own_first, jnp.int32(0))
    new_maxima = jnp.maximum(maxima, jnp.max(jnp.where(allowed, scores, MASKED_SCORE), axis=-1))
    shifted = jnp.where(allowed, jnp.exp(scores - new_maxima[..., None]), 0.0)
    totals = jnp.sum(shifted, axis=-1)
    maxima, totals = (new_maxima, totals)
    log_totals = maxima + jnp.log(totals)
    pieces = (
        lax.all_gather(k_soft, "ctx", axis=0, tiled=True),
        lax.all_gather(v_soft, "ctx", axis=0, tiled=True),
    )
    key_piece = pieces[0].reshape(-1, kv_heads, DH)
    value_piece = pieces[1].reshape(-1, kv_heads, DH)
    scores, allowed = soft_scores(queries, key_piece, own_first, jnp.int32(0))
    soft_rounded = jnp.where(allowed, jnp.exp(scores - log_totals[..., None]), 0.0).astype(
        jnp.bfloat16
    )
    out_full = jnp.einsum(
        "kgrp,pkd->kgrd", soft_rounded, value_piece, preferred_element_type=jnp.float32
    )
    row_dots = jnp.sum(
        jnp.transpose(out_grad.astype(jnp.float32), (1, 2, 0, 3)) * out_full, axis=-1
    )
    o_soft = jnp.transpose(out_full, (2, 0, 1, 3)).reshape(row_count, -1).astype(jnp.bfloat16)
    pieces = (
        lax.all_gather(k_soft, "ctx", axis=0, tiled=True),
        lax.all_gather(v_soft, "ctx", axis=0, tiled=True),
    )
    key_piece = pieces[0].reshape(-1, kv_heads, DH)
    value_piece = pieces[1].reshape(-1, kv_heads, DH)
    soft_rounded, score_grad = back_terms(
        queries, out_grad, key_piece, value_piece, own_first, jnp.int32(0), log_totals, row_dots
    )
    query_grad = jnp.einsum(
        "kgrp,pkd->kgrd", score_grad, key_piece, preferred_element_type=jnp.float32
    )
    total_stats = jnp.transpose(log_totals, (2, 0, 1)).reshape(row_count, -1)
    dot_stats = jnp.transpose(row_dots, (2, 0, 1)).reshape(row_count, -1)
    total_all, dot_all = (
        lax.all_gather(total_stats, "ctx", axis=0, tiled=True),
        lax.all_gather(dot_stats, "ctx", axis=0, tiled=True),
    )
    pieces = (
        lax.all_gather(q_soft, "ctx", axis=0, tiled=True),
        lax.all_gather(g_soft, "ctx", axis=0, tiled=True),
    )
    piece_rows = pieces[0].shape[0]
    query_piece = pieces[0].reshape(piece_rows, kv_heads, group_size, DH)
    grad_piece = pieces[1].reshape(piece_rows, kv_heads, group_size, DH)
    piece_totals = jnp.transpose(total_all.reshape(piece_rows, kv_heads, group_size), (1, 2, 0))
    piece_dots = jnp.transpose(dot_all.reshape(piece_rows, kv_heads, group_size), (1, 2, 0))
    soft_rounded, score_grad = back_terms(
        query_piece,
        grad_piece,
        own_keys,
        own_values,
        jnp.int32(0),
        own_first,
        piece_totals,
        piece_dots,
    )
    key_sum = jnp.einsum(
        "kgrp,rkgd->pkd", score_grad, query_piece, preferred_element_type=jnp.float32
    )
    value_sum = jnp.einsum(
        "kgrp,rkgd->pkd", soft_rounded, grad_piece, preferred_element_type=jnp.float32
    )
    key_sum, value_sum = (key_sum, value_sum)
    key_grad = key_sum.reshape(row_count, -1)
    value_grad = value_sum.reshape(row_count, -1)
    dq_soft = jnp.transpose(query_grad, (2, 0, 1, 3)).reshape(row_count, -1).astype(jnp.bfloat16)
    dk_soft = key_grad.astype(jnp.bfloat16)
    dv_soft = value_grad.astype(jnp.bfloat16)
    return (o_light, dq_light, dk_light, dv_light, o_soft, dq_soft, dk_soft, dv_soft)


def solution(mesh):
    in_specs = (
        P(("dp", "ctx"), "tp"),
        P(("dp", "ctx"), "tp"),
        P(("dp", "ctx"), "tp"),
        P(("dp", "ctx"), "tp"),
        P(("dp", "ctx"), "tp"),
        P(("dp", "ctx"), "tp"),
        P(("dp", "ctx"), "tp"),
        P(("dp", "ctx"), "tp"),
        P(("dp", "ctx"), "tp"),
    )
    out_specs = (
        P(("dp", "ctx"), "tp"),
        P(("dp", "ctx"), "tp"),
        P(("dp", "ctx"), "tp"),
        P(("dp", "ctx"), "tp"),
        P(("dp", "ctx"), "tp"),
        P(("dp", "ctx"), "tp"),
        P(("dp", "ctx"), "tp"),
        P(("dp", "ctx"), "tp"),
    )
    return jax.shard_map(shards, mesh=mesh, in_specs=in_specs, out_specs=out_specs, check_vma=False)
```

profile of v0, /device:TPU:1, one launch (start us, length us, event | category | flops | bytes accessed | tf_op | source)
XLA Modules:
  0.0 642.0 jit_solution(9894644006269180500)
XLA Ops:
  8.0 1.5 copy.136
  9.5 1.7 copy.143
  11.3 1.7 copy.145
  19.5 1.2 fusion.37
  21.4 32.4 %all-gather.4 = f32[32,1,4]{2,1,0:T(1,128)S(1)} all-gather(f32[1,1,4]{2,1,0:T(1,128)S(1)} %slice_bitcast_fusion.1), channel_id=1, replica_groups=mesh['ctx'=32,'tp'=8,'dp'=2] {'ctx'}, dimensions={0}, use_global_device_ids=true | all-gather | bytes 528 | tf_op jit(solution)/shard_map/all_gather | solution.py:15
  57.6 36.2 %all-gather.12.cloned.1.call-done = bf16[4096,128]{1,0:T(8,128)(2,1)} async-done(((bf16[128,128]{1,0:T(8,128)(2,1)}), bf16[4096,128]{1,0:T(8,128)(2,1)}) %all-gather.12.cloned.1.call-update) | async-done | bytes 1048592 | tf_op jit(solution)/shard_map/all_gather | solution.py:139
  93.8 2.5 fusion.8
  96.3 3.2 copy-done.1
  99.5 1.8 fusion.11
  101.3 70.6 %all-gather.14.cloned.1.call-done = bf16[4096,128]{0,1:T(8,128)(2,1)} async-done(((bf16[128,128]{0,1:T(8,128)(2,1)}), bf16[4096,128]{0,1:T(8,128)(2,1)}) %all-gather.14.cloned.1.call-update) | async-done | bytes 1048592 | tf_op jit(solution)/shard_map/all_gather | solution.py:140
  171.9 5.4 multiply_reduce_fusion
  178.1 7.3 %fusion.43 = bf16[4,128,128]{1,2,0:T(8,128)(2,1)S(1)} fusion(f32[4096,128,4]{1,0,2:T(8,128)} %copy-done.1, f32[4,128]{1,0:T(4,128)S(1)} %get-tuple-element.310, f32[4,128]{1,0:T(4,128)S(1)} %log_add_fusion, pred[128,4096]{0,1:T(8,128)(4,1)S(1)} %iota_compare_fusion.1, bf16[4096,128]{0,1:T(8,128)(2,1)} %all-gather.14.cloned.1.call-done, ...), kind=kOutput, calls=%fused_computation.62 | convolution fusion | flops 1088487424 | bytes 11276288 | tf_op jit(solution)/shard_map/kgrp,pkd->kgrd/dot_general | solution.py:164
  186.1 36.9 %all-gather.2 = f32[4096,1,4]{0,2,1:T(4,128)S(1)} all-gather(f32[128,1,4]{0,2,1:T(4,128)S(1)} %bitcast.335), channel_id=4, replica_groups=mesh['ctx'=32,'tp'=8,'dp'=2] {'ctx'}, dimensions={0}, use_global_device_ids=true | all-gather | bytes 67584 | tf_op jit(solution)/shard_map/all_gather | solution.py:170
  223.0 39.2 %all-gather.3 = f32[4096,1,4]{0,2,1:T(4,128)S(1)} all-gather(f32[128,1,4]{0,2,1:T(4,128)S(1)} %bitcast.336), channel_id=5, replica_groups=mesh['ctx'=32,'tp'=8,'dp'=2] {'ctx'}, dimensions={0}, use_global_device_ids=true | all-gather | bytes 67584 | tf_op jit(solution)/shard_map/all_gather | solution.py:171
  262.2 2.2 all-gather.16.cloned.1.call-done
  264.4 8.1 %fusion.5 = f32[1,4,4096,128]{2,3,1,0:T(8,128)} fusion(bf16[4096,4,128]{0,2,1:T(8,128)(2,1)} %bitcast.307, f32[4,4096]{1,0:T(4,128)S(1)} %bitcast.328, pred[4096,128]{0,1:T(8,128)(4,1)S(1)} %iota_compare_fusion, bf16[128,128]{1,0:T(8,128)(2,1)S(1)} %copy-done.4), kind=kOutput, calls=%fused_computation.11 | convolution fusion | flops 543162368 | bytes 13205504 | tf_op jit(solution)/shard_map/rkgd,pkd->kgrp/dot_general | solution.py:96
  272.5 84.4 %all-gather.18.cloned.1.call-done = bf16[4096,512]{0,1:T(8,128)(2,1)} async-done(((bf16[128,512]{0,1:T(8,128)(2,1)}), bf16[4096,512]{0,1:T(8,128)(2,1)}) %all-gather.18.cloned.1.call-update) | async-done | bytes 4194320 | tf_op jit(solution)/shard_map/all_gather | solution.py:175
  356.9 6.4 %fusion.48 = bf16[128,128]{1,0:T(8,128)(2,1)} fusion(bf16[4096,4,128]{0,2,1:T(8,128)(2,1)} %bitcast.309, f32[1,4,4096,128]{2,3,1,0:T(8,128)} %fusion.5), kind=kOutput, calls=%fused_computation.65 | convolution fusion | flops 538984448 | bytes 12615680 | tf_op jit(solution)/shard_map/kgrp,rkgd->pkd/dot_general | solution.py:195
  363.3 8.8 %fusion.51 = bf16[128,128]{1,0:T(8,128)(2,1)} fusion(bf16[4096,4,128]{0,2,1:T(8,128)(2,1)} %bitcast.308, bf16[4096,4,128]{0,2,1:T(8,128)(2,1)} %bitcast.310, f32[1,4,4096,128]{2,3,1,0:T(8,128)} %fusion.5, f32[4,4096]{1,0:T(4,128)S(1)} %bitcast.327, bf16[128,128]{1,0:T(8,128)(2,1)S(1)} %copy-done.5), kind=kOutput, calls=%fused_computation.66 | convolution fusion | flops 1082146816 | bytes 16908288 | tf_op jit(solution)/shard_map/kgrp,rkgd->pkd/dot_general | solution.py:192
  372.1 94.4 %all-gather.20.cloned.1.call-done = f32[128,128,128]{2,1,0:T(8,128)} async-done(((f32[4,128,128]{2,1,0:T(8,128)}), f32[128,128,128]{2,1,0:T(8,128)}) %all-gather.20.cloned.1.call-update) | async-done | bytes 8388624 | tf_op jit(solution)/shard_map/all_gather | solution.py:15
  466.6 54.6 %while.28 = (s32[]{:T(128)}, f32[4,128,128]{2,1,0:T(8,128)S(1)}, s32[]{:T(128)}, f32[32,4]{1,0:T(8,128)}, f32[32,4,128,128]{3,2,1,0:T(8,128)}, /*index=5*/s32[]{:T(128)}, s32[]{:T(128)}) while((s32[]{:T(128)}, f32[4,128,128]{2,1,0:T(8,128)S(1)}, s32[]{:T(128)}, f32[32,4]{1,0:T(8,128)}, f32[32,4,128,128]{3,2,1,0:T(8,128)}, ...), condition=%wide.region_2.3_spmd.clone, body=%wide.region_1.2_spmd.clone.sunk | while | flops 262148 | bytes 786593 | solution.py:27
  523.4 47.2 %all-gather.22.cloned.1.call-done = f32[128,128,128]{2,1,0:T(8,128)} async-done(((f32[4,128,128]{2,1,0:T(8,128)}), f32[128,128,128]{2,1,0:T(8,128)}) %all-gather.22.cloned.1.call-update) | async-done | bytes 8388624 | tf_op jit(solution)/shard_map/all_gather | solution.py:15
  570.6 7.8 %rev.7 = f32[32,4,128,128]{3,2,1,0:T(8,128)} reverse(f32[32,4,128,128]{3,2,1,0:T(8,128)} %bitcast.311), dimensions={0} | reverse | bytes 16777216 | tf_op jit(solution)/shard_map/rev | solution.py:17
  578.4 54.4 %while.29 = (s32[]{:T(128)}, f32[4,128,128]{2,1,0:T(8,128)S(1)}, s32[]{:T(128)}, f32[32,4]{1,0:T(8,128)}, f32[32,4,128,128]{3,2,1,0:T(8,128)}, /*index=5*/s32[]{:T(128)}, s32[]{:T(128)}) while((s32[]{:T(128)}, f32[4,128,128]{2,1,0:T(8,128)S(1)}, s32[]{:T(128)}, f32[32,4]{1,0:T(8,128)}, f32[32,4,128,128]{3,2,1,0:T(8,128)}, ...), condition=%wide.region_4.5_spmd.clone, body=%wide.region_3.4_spmd.clone.sunk | while | flops 262148 | bytes 786593 | solution.py:27
  (192 shorter events, 125.8 us)
Async XLA Ops:
  7.2 7.9 %copy-start = (bf16[128,512]{1,0:T(8,128)(2,1)S(1)}, bf16[128,512]{1,0:T(8,128)(2,1)}, u32[]{:S(2)}) copy-start(bf16[128,512]{1,0:T(8,128)(2,1)} %param.15) | copy-start | bytes 393220
  7.2 86.6 %copy-start.6 = (bf16[128,512]{1,0:T(8,128)(2,1)S(1)}, bf16[128,512]{1,0:T(8,128)(2,1)}, u32[]{:S(2)}) copy-start(bf16[128,512]{1,0:T(8,128)(2,1)} %param.18) | copy-start | bytes 393220
  7.2 86.6 %all-gather.12.cloned.1.call-start = ((), (), s32[]{:S(2)}) async-start(), calls=%async_computation | async-start | bytes 1081344 | tf_op jit(solution)/shard_map/all_gather | solution.py:139
  7.9 164.0 %all-gather.14.cloned.1.call-start = ((), (), s32[]{:S(2)}) async-start(), calls=%async_computation.1 | async-start | bytes 1081344 | tf_op jit(solution)/shard_map/all_gather | solution.py:140
  9.5 254.9 %all-gather.16.cloned.1.call-start = ((), (), s32[]{:S(2)}) async-start(), calls=%async_computation.2 | async-start | bytes 4325376 | tf_op jit(solution)/shard_map/all_gather | solution.py:174
  11.2 345.6 %all-gather.18.cloned.1.call-start = ((), (), s32[]{:S(2)}) async-start(), calls=%async_computation.3 | async-start | bytes 4325376 | tf_op jit(solution)/shard_map/all_gather | solution.py:175
  13.0 453.6 %all-gather.20.cloned.1.call-start = ((), (), s32[]{:S(2)}) async-start(), calls=%async_computation.4 | async-start | bytes 8650752 | tf_op jit(solution)/shard_map/all_gather | solution.py:15
  16.1 554.5 %all-gather.22.cloned.1.call-start = ((), (), s32[]{:S(2)}) async-start(), calls=%async_computation.5 | async-start | bytes 8650752 | tf_op jit(solution)/shard_map/all_gather | solution.py:15
  96.3 3.2 copy-start.1
  101.3 76.8 %copy-start.2 = (bf16[128,512]{1,0:T(8,128)(2,1)S(1)}, bf16[128,512]{1,0:T(8,128)(2,1)}, u32[]{:S(2)}) copy-start(bf16[128,512]{1,0:T(8,128)(2,1)} %param.21) | copy-start | bytes 393220
  178.1 86.3 %copy-start.4 = (bf16[128,128]{1,0:T(8,128)(2,1)S(1)}, bf16[128,128]{1,0:T(8,128)(2,1)}, u32[]{:S(2)}) copy-start(bf16[128,128]{1,0:T(8,128)(2,1)} %param.19) | copy-start | bytes 98308
  272.5 90.8 %copy-start.5 = (bf16[128,128]{1,0:T(8,128)(2,1)S(1)}, bf16[128,128]{1,0:T(8,128)(2,1)}, u32[]{:S(2)}) copy-start(bf16[128,128]{1,0:T(8,128)(2,1)} %param.20) | copy-start | bytes 98308
  570.6 63.3 %copy-start.3 = (bf16[128,512]{1,0:T(8,128)(2,1)S(1)}, bf16[128,512]{1,0:T(8,128)(2,1)}, u32[]{:S(2)}) copy-start(bf16[128,512]{1,0:T(8,128)(2,1)} %param.14) | copy-start | bytes 393220
Sparse Core Ops, SparseCore 0:
  11.2 82.5 all-gather.11
  97.4 74.4 all-gather.13
  175.5 88.7 all-gather.15
  267.8 88.9 all-gather.17
  359.9 106.6 all-gather.19
  469.6 100.9 all-gather.21
where the time goes:
time: 646 us; the launch traced here: 642 us
  waiting for transfers between devices  336 us (52%)
  blocking collectives  108 us (17%)
  local copies, waits for them, and re-layouts  70.1 us (11%)
  other arithmetic  67.8 us (10%)
  matrix products  44.2 us (7%)
  between operations  14.4 us (2%)
    all_gather x2, waiting for transfers between devices, prefix(): pieces = jax.tree.map(lambda part: lax.all_gather(part, axis), value)  142 us
    all_gather x1, waiting for transfers between devices, shards(): lax.all_gather(g_soft, 'ctx', axis=0, tiled=True)  84.4 us
    all_gather x1, waiting for transfers between devices, shards(): lax.all_gather(v_soft, 'ctx', axis=0, tiled=True)  70.6 us
    select_n x62, other arithmetic, turn(): jnp.where(position < mine, new, old)  65 us
    mul x62, local copies, waits for them, and re-layouts, combine_states(): later[0][:, None, None] * earlier[1] + later[1]  42.9 us
    all_gather x1, blocking collectives, shards(): lax.all_gather(dot_stats, 'ctx', axis=0, tiled=True)  39.2 us
    all_gather x1, blocking collectives, shards(): lax.all_gather(total_stats, 'ctx', axis=0, tiled=True)  36.9 us
    all_gather x1, waiting for transfers between devices, shards(): lax.all_gather(k_soft, 'ctx', axis=0, tiled=True)  36.2 us
  transfers between devices with their start and end apart: 6, of which 6 were waited for; matrix products, arithmetic and copies ran while one was open for 18% of the time, Pallas kernels for 0%

commit v1 on v0

v1 whole, which is shorter than its diff:
```python
import jax
import jax.numpy as jnp
from jax import lax
from jax.experimental import pallas as pl
from jax.experimental.pallas import tpu as pltpu
from jax.sharding import PartitionSpec as P

DH = 128
ROWS = 128
NX = 4
NY = 8
HEADS = 4
WIDE = HEADS * DH
SPAN = NX * ROWS
CHUNK = 64
SCALE = DH**-0.5
LOG2E = 1.4426950408889634
MASKED = -1e30
F32 = jnp.float32
BF16 = jnp.bfloat16


def mm(a, b):
    return jnp.dot(a, b, preferred_element_type=F32)


def mm_nt(a, b):
    return lax.dot_general(a, b, (((1,), (1,)), ((), ())), preferred_element_type=F32)


def mm_tn(a, b):
    return lax.dot_general(a, b, (((0,), (0,)), ((), ())), preferred_element_type=F32)


def push(src, dst, send, recv, target):
    return pltpu.make_async_remote_copy(
        src_ref=src,
        dst_ref=dst,
        send_sem=send,
        recv_sem=recv,
        device_id={"ctx": target},
        device_id_type=pl.DeviceIdType.MESH,
    )


def split_log(total):
    high = total.astype(BF16)
    rest = total - high.astype(F32)
    middle = rest.astype(BF16)
    low = (rest - middle.astype(F32)).astype(BF16)
    return high, middle, low


def join_log(ref, first):
    return (
        ref[first : first + 16, :].astype(F32)
        + ref[first + 16 : first + 32, :].astype(F32)
        + ref[first + 32 : first + 48, :].astype(F32)
    )[0:1, :]


def kernel(
    q_l, k_l, v_l, g_l, ld, q_s, k_s, v_s, g_s,
    o_l, dq_l, dk_l, dv_l, o_s, dq_s, dk_s, dv_s,
    qs, gs, kg, vg, e_ref, dp_ref, stat_m, stat_l, stat_t, dot_ref, wb_ref, ds_ref,
    out_t, dq_t, dkf, dkp, rbuf, dvp, vr, vsum, vfin, kfin, dks,
    lall, intra, lmsg, lin, ymsg, yin, cp, cg, lout, fin,
    kx_s, kx_r, kr_s, kr_r, vy_s, vy_r, vx_s, vx_r,
    l1_s, l1_r, y_s, y_r, l3_s, l3_r,
    dr_s, dr_r, du_s, du_r, dw_s, dw_r, kf_s, kf_r,
):
    me = lax.axis_index("ctx")
    y = lax.div(me, NX)
    x = lax.rem(me, NX)
    sigma = 1 - 2 * lax.rem(lax.axis_index("tp"), 2)

    def ring(value):
        return lax.rem(value + 2 * NY, NY)

    def at(yy, xx):
        return yy * NX + xx

    def col(step):
        return lax.rem(x + step + NX, NX)

    barrier = pltpu.get_barrier_semaphore()
    for dx in range(1, NX):
        pl.semaphore_signal(
            barrier, inc=1, device_id={"ctx": at(y, col(dx))},
            device_id_type=pl.DeviceIdType.MESH,
        )
    for dy in range(1, NY):
        pl.semaphore_signal(
            barrier, inc=1, device_id={"ctx": at(ring(y + dy), x)},
            device_id_type=pl.DeviceIdType.MESH,
        )
    pl.semaphore_wait(barrier, NX + NY - 2)

    def key_across(dx, owner):
        return push(k_s, kg.at[y, owner], kx_s.at[dx - 1], kx_r.at[dx - 1], at(y, col(dx)))

    def value_along(dy, owner):
        return push(
            v_s, vg.at[owner, x], vy_s.at[dy - 1], vy_r.at[dy - 1],
            at(jnp.minimum(y + dy, NY - 1), x),
        )

    def value_across(dy, dx, row, owner):
        return push(
            vg.at[row, x], vg.at[row, owner], vx_s.at[dy, dx - 1], vx_r.at[dy, dx - 1],
            at(y, col(dx)),
        )

    def key_ring(place, row, turn):
        return push(kg.at[row], kg.at[row], kr_s.at[place], kr_r.at[place], at(ring(y + turn), x))

    for dx in range(1, NX):
        key_across(dx, x).start()
    for dy in range(1, NY):
        @pl.when(y + dy < NY)
        def _():
            value_along(dy, y).start()
    kg[y, x] = k_s[...]
    vg[y, x] = v_s[...]
    for dx in range(1, NX):
        value_across(0, dx, y, x).start()

    for h in range(HEADS):
        part = slice(h * DH, (h + 1) * DH)
        qs[part, :] = q_s[:, part]
        gs[part, :] = g_s[:, part]
    for r in range(NY):
        stat_m[r] = jnp.full((8, WIDE), MASKED, F32)
        stat_l[r] = jnp.zeros((8, WIDE), F32)
        stat_t[r] = jnp.zeros((8, WIDE), F32)
    out_t[...] = jnp.zeros_like(out_t)
    dq_t[...] = jnp.zeros_like(dq_t)
    cp[...] = jnp.zeros_like(cp)
    cg[...] = jnp.zeros_like(cg)

    def soft_row(r, masked):
        top = jnp.full((8, WIDE), MASKED, F32)
        for b in range(NX):
            scores = mm_nt(kg[r, b], qs[...])
            if masked:
                key_at = lax.broadcasted_iota(jnp.int32, (ROWS, WIDE), 0) + b * ROWS
                query_at = lax.rem(lax.broadcasted_iota(jnp.int32, (ROWS, WIDE), 1), ROWS)
                scores = jnp.where(key_at <= query_at + x * ROWS, scores, MASKED)
            e_ref[r, b * ROWS : (b + 1) * ROWS, :] = scores
            top = jnp.maximum(top, jnp.max(scores.reshape(ROWS // 8, 8, WIDE), axis=0))
        top = jnp.max(top, axis=0, keepdims=True)
        stat_m[r] = jnp.broadcast_to(top, (8, WIDE))
        shift = top * (SCALE * LOG2E)

        def turn(i, total):
            rows = pl.ds(pl.multiple_of(i * CHUNK, CHUNK), CHUNK)
            grown = jnp.exp2(e_ref[r, rows, :] * (SCALE * LOG2E) - shift)
            e_ref[r, rows, :] = grown
            return total + jnp.sum(grown.reshape(CHUNK // 8, 8, WIDE), axis=0)

        total = lax.fori_loop(0, SPAN // CHUNK, turn, jnp.zeros((8, WIDE), F32))
        stat_l[r] = jnp.broadcast_to(jnp.sum(total, axis=0, keepdims=True), (8, WIDE))

    def light_head(h):
        cols = pl.ds(pl.multiple_of(h * DH, DH), DH)
        qh, kh, vh, gh = q_l[:, cols], k_l[:, cols], v_l[:, cols], g_l[:, cols]
        level = lall[:, cols]
        row_at = lax.broadcasted_iota(jnp.int32, (ROWS, ROWS), 0)
        causal = row_at >= lax.broadcasted_iota(jnp.int32, (ROWS, ROWS), 1)
        gaps = jnp.where(causal, level - level.T, 0.0)
        weights = jnp.where(causal, jnp.exp(gaps), 0.0) * SCALE
        mixing = (mm_nt(qh, kh) * weights).astype(BF16)
        back_mix = (mm_nt(gh, vh) * weights).astype(BF16)
        intra[0, :, cols] = mm(mixing, vh)
        intra[1, :, cols] = mm(back_mix, kh)
        intra[2, :, cols] = mm_tn(back_mix, qh)
        intra[3, :, cols] = mm_tn(mixing, gh)
        last = level[ROWS - 1 : ROWS, :]
        fading = (kh.astype(F32) * jnp.exp(last - level)).astype(BF16)
        entering = (qh.astype(F32) * jnp.exp(level)).astype(BF16)
        lmsg[h, 0:DH, :] = mm_tn(fading, vh).astype(BF16)
        lmsg[h, DH : 2 * DH, :] = mm_tn(entering, gh).astype(BF16)
        for n, term in enumerate(split_log(jnp.broadcast_to(last, (16, DH)))):
            lmsg[h, 2 * DH + 16 * n : 2 * DH + 16 * (n + 1), :] = term

    def light_send(h, owner):
        return push(lmsg.at[h], lin.at[owner], l1_s.at[h], l1_r.at[owner], at(y, h))

    for dx in range(1, NX):
        key_across(dx, col(-dx)).wait_recv()
    key_ring(1, y, sigma).start()
    key_ring(2, y, -sigma).start()
    soft_row(y, True)

    spread = jnp.concatenate(
        [jnp.broadcast_to(ld[:, h : h + 1], (ROWS, DH)) for h in range(HEADS)], axis=1
    )
    lower = (
        lax.broadcasted_iota(jnp.int32, (ROWS, ROWS), 0)
        >= lax.broadcasted_iota(jnp.int32, (ROWS, ROWS), 1)
    ).astype(F32)
    lall[...] = jnp.dot(
        lower, spread, precision=lax.Precision.HIGHEST, preferred_element_type=F32
    )

    def gather_turn(place, _):
        turn = sigma * (2 * lax.rem(place, 2) - 1)
        row = ring(y - turn * lax.div(place + 1, 2))
        key_ring(place, row, turn).wait_recv()

        @pl.when(place <= NY - 3)
        def _():
            key_ring(place + 2, row, turn).start()

        @pl.when(y - place >= 0)
        def _():
            push(
                v_s, vg.at[y - place, x], vy_s.at[place - 1], vy_r.at[place - 1], at(y - place, x)
            ).wait_recv()
            for dx in range(1, NX):
                value_across(place, dx, y - place, x).start()

        @pl.when(place <= HEADS)
        def _():
            h = place - 1
            light_head(h)

            @pl.when(h != x)
            def _():
                light_send(h, x).start()

            @pl.when(h == x)
            def _():
                lin[x] = lmsg[h]

        @pl.when(row < y)
        def _():
            soft_row(row, False)

        return 0

    lax.fori_loop(1, NY, gather_turn, 0)

    for h in range(NX):
        @pl.when(h != x)
        def _():
            push(lmsg.at[h], lin.at[h], l1_s.at[h], l1_r.at[h], at(y, h)).wait_recv()
    levels = [join_log(lin.at[b], 2 * DH) for b in range(NX)]
    row_state = lin[0, 0:DH, :].astype(F32)
    for b in range(1, NX):
        row_state = jnp.exp(levels[b]) * row_state + lin[b, 0:DH, :].astype(F32)
    row_grad = lin[NX - 1, DH : 2 * DH, :].astype(F32)
    for b in range(NX - 2, -1, -1):
        row_grad = jnp.exp(levels[b]) * row_grad + lin[b, DH : 2 * DH, :].astype(F32)
    row_level = jnp.broadcast_to(levels[0] + levels[1] + levels[2] + levels[3], (16, DH))
    ymsg[0, 0:DH, :] = row_state.astype(BF16)
    ymsg[1, 0:DH, :] = row_grad.astype(BF16)
    for n, term in enumerate(split_log(row_level)):
        ymsg[0, DH + 16 * n : DH + 16 * (n + 1), :] = term
        ymsg[1, DH + 16 * n : DH + 16 * (n + 1), :] = term

    def state_along(dy, owner):
        kind = jnp.where(y + dy < NY, 0, 1)
        return push(
            ymsg.at[kind], yin.at[owner], y_s.at[dy - 1], y_r.at[dy - 1], at(ring(y + dy), x)
        )

    for dy in range(1, NY):
        state_along(dy, y).start()

    def value_turn(dy, _):
        row = y - dy
        for dx in range(1, NX):
            value_across(dy, dx, row, col(-dx)).wait_recv()
        total = jnp.zeros((8, WIDE), F32)
        for b in range(NX):
            grads = mm_nt(vg[row, b], gs[...])
            dp_ref[row, b * ROWS : (b + 1) * ROWS, :] = grads
            weighed = grads * e_ref[row, b * ROWS : (b + 1) * ROWS, :]
            total = total + jnp.sum(weighed.reshape(ROWS // 8, 8, WIDE), axis=0)
        stat_t[row] = jnp.broadcast_to(jnp.sum(total, axis=0, keepdims=True), (8, WIDE))
        return 0

    lax.fori_loop(0, y + 1, value_turn, 0)

    top = stat_m[0]
    for r in range(1, NY):
        top = jnp.maximum(top, stat_m[r])
    total = jnp.zeros((8, WIDE), F32)
    dots = jnp.zeros((8, WIDE), F32)
    for r in range(NY):
        factor = jnp.exp2((stat_m[r] - top) * (SCALE * LOG2E))
        total = total + factor * stat_l[r]
        dots = dots + factor * stat_t[r]
        stat_m[r] = factor
    inverse = 1.0 / total
    dot_ref[...] = dots * inverse
    for r in range(NY):
        stat_l[r] = stat_m[r] * inverse

    for dy in range(1, NY):
        state_along(dy, ring(y - dy)).wait_recv()
    for yy in range(NY):
        @pl.when(yy < y)
        def _():
            cp[...] = jnp.exp(join_log(yin.at[yy], DH)) * cp[...] + yin[yy, 0:DH, :].astype(F32)
    for yy in range(NY - 1, -1, -1):
        @pl.when(yy > y)
        def _():
            cg[...] = jnp.exp(join_log(yin.at[yy], DH)) * cg[...] + yin[yy, 0:DH, :].astype(F32)
    carried = cp[...]
    for b in range(NX):
        lout[b, 0:DH, :] = carried.astype(BF16)
        carried = jnp.exp(join_log(lin.at[b], 2 * DH)) * carried + lin[b, 0:DH, :].astype(F32)
    carried = cg[...]
    for b in range(NX - 1, -1, -1):
        lout[b, DH : 2 * DH, :] = carried.astype(BF16)
        carried = jnp.exp(join_log(lin.at[b], 2 * DH)) * carried + lin[b, DH : 2 * DH, :].astype(F32)

    def state_back(b, owner):
        return push(lout.at[b], fin.at[owner], l3_s.at[b], l3_r.at[owner], at(y, b))

    for b in range(NX):
        @pl.when(b != x)
        def _():
            state_back(b, x).start()
    fin[x] = lout[x]

    def grad_ring(place, turn):
        return push(
            dkp.at[place], rbuf.at[place], dr_s.at[place], dr_r.at[place], at(ring(y + turn), x)
        )

    def dv_across(row, dx):
        return push(
            dvp.at[row, col(dx)], vr.at[row, dx - 1], du_s.at[row, dx - 1], du_r.at[row, dx - 1],
            at(y, col(dx)),
        )

    def dv_along(row, owner):
        return push(vsum.at[row], vfin.at[owner], dw_s.at[row], dw_r.at[owner], at(row, x))

    def dv_sum(row):
        for dx in range(1, NX):
            dv_across(row, dx).wait_recv()
        return (
            dvp[row, x].astype(F32)
            + vr[row, 0].astype(F32)
            + vr[row, 1].astype(F32)
            + vr[row, 2].astype(F32)
        )

    def place_row(place):
        forth = (lax.rem(place, 2) == 1) | (place == 0)
        turn = jnp.where(forth, sigma, -sigma)
        return turn, ring(y + turn * (4 - lax.div(place + 1, 2)))

    def back_turn(place, _):
        turn, row = place_row(place)

        @pl.when(row <= y)
        def _():
            def weigh(i, _):
                rows = pl.ds(pl.multiple_of(i * CHUNK, CHUNK), CHUNK)
                weights = e_ref[row, rows, :] * stat_l[row, 0:1, :]
                wb_ref[rows, :] = weights.astype(BF16)
                ds_ref[rows, :] = (weights * (dp_ref[row, rows, :] - dot_ref[0:1, :])).astype(BF16)
                return 0

            lax.fori_loop(0, SPAN // CHUNK, weigh, 0)
            dvp[row] = mm(wb_ref[...], gs[...]).astype(BF16).reshape(NX, ROWS, DH)
            for dx in range(1, NX):
                dv_across(row, dx).start()
            dkf[...] = (mm(ds_ref[...], qs[...]) * SCALE).reshape(NX, ROWS, DH)

        @pl.when(row > y)
        def _():
            dkf[...] = jnp.zeros_like(dkf)

        @pl.when((place != 0) & (place != 2) & (place != NY - 1))
        def _():
            before = jnp.where(place == 1, 0, place - 2)
            grad_ring(before, turn).wait_recv()
            dkf[...] += rbuf[before].astype(F32)

        @pl.when(place < NY - 1)
        def _():
            dkp[place] = dkf[...].astype(BF16)
            grad_ring(place, turn).start()

        @pl.when(row <= y)
        def _():
            out_t[...] += mm_tn(vg[row].reshape(SPAN, DH), wb_ref[...])
            dq_t[...] += mm_tn(kg[row].reshape(SPAN, DH), ds_ref[...])

        @pl.when(place >= 1)
        def _():
            _, before_row = place_row(place - 1)

            @pl.when(before_row < y)
            def _():
                vsum[before_row] = dv_sum(before_row).astype(BF16)
                dv_along(before_row, y).start()

        return 0

    lax.fori_loop(0, NY, back_turn, 0)

    for b in range(NX):
        @pl.when(b != x)
        def _():
            push(lout.at[b], fin.at[b], l3_s.at[b], l3_r.at[b], at(y, b)).wait_recv()

    def light_out(h, _):
        cols = pl.ds(pl.multiple_of(h * DH, DH), DH)
        qh, kh, vh, gh = q_l[:, cols], k_l[:, cols], v_l[:, cols], g_l[:, cols]
        level = lall[:, cols]
        entering = jnp.exp(level) * SCALE
        fading = jnp.exp(level[ROWS - 1 : ROWS, :] - level) * SCALE
        prior = fin[h, 0:DH, :]
        later = fin[h, DH : 2 * DH, :]
        o_l[:, cols] = (intra[0, :, cols] + entering * mm(qh, prior)).astype(BF16)
        dq_l[:, cols] = (intra[1, :, cols] + entering * mm_nt(gh, prior)).astype(BF16)
        dk_l[:, cols] = (intra[2, :, cols] + fading * mm_nt(vh, later)).astype(BF16)
        dv_l[:, cols] = (intra[3, :, cols] + fading * mm(kh, later)).astype(BF16)
        return 0

    lax.fori_loop(0, HEADS, light_out, 0)

    grad_ring(NY - 3, sigma).wait_recv()
    grad_ring(NY - 2, sigma).wait_recv()
    dkf[...] += rbuf[NY - 3].astype(F32) + rbuf[NY - 2].astype(F32)
    dks[...] = dkf[...].astype(BF16)

    def dk_across(dx):
        return push(
            dks.at[col(dx)], kfin.at[dx - 1], kf_s.at[dx - 1], kf_r.at[dx - 1], at(y, col(dx))
        )

    for dx in range(1, NX):
        dk_across(dx).start()

    for h in range(HEADS):
        part = slice(h * DH, (h + 1) * DH)
        o_s[:, part] = out_t[:, part].T.astype(BF16)
        dq_s[:, part] = (dq_t[:, part].T * SCALE).astype(BF16)

    cp[...] = dv_sum(y)
    for yy in range(1, NY):
        @pl.when(yy > y)
        def _():
            push(vsum.at[yy], vfin.at[yy], dw_s.at[yy], dw_r.at[yy], at(yy, x)).wait_recv()
            cp[...] += vfin[yy].astype(F32)
    dv_s[...] = cp[...].astype(BF16)

    for dx in range(1, NX):
        dk_across(dx).wait_recv()
    dk_s[...] = (
        dkf[x] + kfin[0].astype(F32) + kfin[1].astype(F32) + kfin[2].astype(F32)
    ).astype(BF16)

    for dx in range(1, NX):
        key_across(dx, x).wait_send()
        dk_across(dx).wait_send()
    for dy in range(1, NY):
        state_along(dy, y).wait_send()
        key_ring(dy, y, sigma).wait_send()
        grad_ring(dy - 1, sigma).wait_send()

        @pl.when(y + dy < NY)
        def _():
            value_along(dy, y).wait_send()

        @pl.when(dy - 1 < y)
        def _():
            dv_along(dy - 1, y).wait_send()
    for b in range(NX):
        @pl.when(b != x)
        def _():
            light_send(b, x).wait_send()
            state_back(b, x).wait_send()
    for dy in range(NY):
        @pl.when(dy <= y)
        def _():
            for dx in range(1, NX):
                value_across(dy, dx, y, x).wait_send()
                dv_across(dy, dx).wait_send()


def shards(q_light, k_light, v_light, g_light, log_decay, q_soft, k_soft, v_soft, g_soft):
    dma = pltpu.SemaphoreType.DMA
    wide = jax.ShapeDtypeStruct((ROWS, WIDE), BF16)
    narrow = jax.ShapeDtypeStruct((ROWS, DH), BF16)
    scratch = [
        pltpu.VMEM((WIDE, DH), BF16),
        pltpu.VMEM((WIDE, DH), BF16),
        pltpu.VMEM((NY, NX, ROWS, DH), BF16),
        pltpu.VMEM((NY, NX, ROWS, DH), BF16),
        pltpu.VMEM((NY, SPAN, WIDE), F32),
        pltpu.VMEM((NY, SPAN, WIDE), F32),
        pltpu.VMEM((NY, 8, WIDE), F32),
        pltpu.VMEM((NY, 8, WIDE), F32),
        pltpu.VMEM((NY, 8, WIDE), F32),
        pltpu.VMEM((8, WIDE), F32),
        pltpu.VMEM((SPAN, WIDE), BF16),
        pltpu.VMEM((SPAN, WIDE), BF16),
        pltpu.VMEM((DH, WIDE), F32),
        pltpu.VMEM((DH, WIDE), F32),
        pltpu.VMEM((NX, ROWS, DH), F32),
        pltpu.VMEM((NY - 1, NX, ROWS, DH), BF16),
        pltpu.VMEM((NY - 1, NX, ROWS, DH), BF16),
        pltpu.VMEM((NY, NX, ROWS, DH), BF16),
        pltpu.VMEM((NY, NX - 1, ROWS, DH), BF16),
        pltpu.VMEM((NY, ROWS, DH), BF16),
        pltpu.VMEM((NY, ROWS, DH), BF16),
        pltpu.VMEM((NX - 1, ROWS, DH), BF16),
        pltpu.VMEM((NX, ROWS, DH), BF16),
        pltpu.VMEM((ROWS, WIDE), F32),
        pltpu.VMEM((4, ROWS, WIDE), F32),
        pltpu.VMEM((HEADS, 2 * DH + 48, DH), BF16),
        pltpu.VMEM((NX, 2 * DH + 48, DH), BF16),
        pltpu.VMEM((2, DH + 48, DH), BF16),
        pltpu.VMEM((NY, DH + 48, DH), BF16),
        pltpu.VMEM((DH, DH), F32),
        pltpu.VMEM((DH, DH), F32),
        pltpu.VMEM((NX, 2 * DH, DH), BF16),
        pltpu.VMEM((HEADS, 2 * DH, DH), BF16),
        dma((NX - 1,)), dma((NX - 1,)),
        dma((NY,)), dma((NY,)),
        dma((NY - 1,)), dma((NY - 1,)),
        dma((NY, NX - 1)), dma((NY, NX - 1)),
        dma((NX,)), dma((NX,)),
        dma((NY - 1,)), dma((NY - 1,)),
        dma((NX,)), dma((NX,)),
        dma((NY - 1,)), dma((NY - 1,)),
        dma((NY, NX - 1)), dma((NY, NX - 1)),
        dma((NY,)), dma((NY,)),
        dma((NX - 1,)), dma((NX - 1,)),
    ]
    vmem = pl.BlockSpec(memory_space=pltpu.VMEM)
    return pl.pallas_call(
        kernel,
        out_shape=(wide, wide, wide, wide, wide, wide, narrow, narrow),
        in_specs=[vmem] * 9,
        out_specs=(vmem,) * 8,
        scratch_shapes=scratch,
        compiler_params=pltpu.CompilerParams(
            collective_id=0, has_side_effects=True, vmem_limit_bytes=48 * 1024 * 1024
        ),
    )(q_light, k_light, v_light, g_light, log_decay, q_soft, k_soft, v_soft, g_soft)


def solution(mesh):
    spec = P(("dp", "ctx"), "tp")
    return jax.shard_map(
        shards, mesh=mesh, in_specs=(spec,) * 9, out_specs=(spec,) * 8, check_vma=False
    )
```

time: 646 us -> 81.9 us (0.13)
  the two profiles are of different devices: /device:TPU:1 before, /device:TPU:392 now
where the time goes in v1:
time: 81.9 us; the launch traced here: 81.6 us
  Pallas kernels  69.6 us (85%)
  local copies, waits for them, and re-layouts  11.4 us (14%)
    pallas_call x1, Pallas kernels, shards(): pl.pallas_call(kernel, out_shape=(wide, wide, wide, wide, wide, wide, nar...  69.6 us
    unnamed x25, local copies, waits for them, and re-layouts  11.4 us

profile of v1, /device:TPU:392, one launch (start us, length us, event | category | flops | bytes accessed | tf_op | source)
XLA Modules:
  0.0 81.6 jit_solution(4017020527167509952)
XLA Ops:
  0.6 0.0 copy-start.7
  0.6 0.0 copy-start.6
  0.7 0.8 copy.17.ld
  1.5 0.0 copy-done.7
  1.5 0.0 copy-done.6
  1.5 0.0 copy-start
  1.5 0.9 %copy-done = bf16[128,512]{1,0:T(8,128)(2,1)S(1)} copy-done((bf16[128,512]{1,0:T(8,128)(2,1)S(1)}, bf16[128,512]{1,0:T(8,128)(2,1)}, u32[]{:S(2)}) %copy-start) | copy-done | bytes 131096
  2.4 0.0 copy-start.1
  2.4 0.9 %copy-done.1 = bf16[128,512]{1,0:T(8,128)(2,1)S(1)} copy-done((bf16[128,512]{1,0:T(8,128)(2,1)S(1)}, bf16[128,512]{1,0:T(8,128)(2,1)}, u32[]{:S(2)}) %copy-start.1) | copy-done | bytes 131096
  3.3 0.0 copy-start.2
  3.3 0.9 %copy-done.2 = bf16[128,512]{1,0:T(8,128)(2,1)S(1)} copy-done((bf16[128,512]{1,0:T(8,128)(2,1)S(1)}, bf16[128,512]{1,0:T(8,128)(2,1)}, u32[]{:S(2)}) %copy-start.2) | copy-done | bytes 131096
  4.2 0.9 %copy-done.3 = bf16[128,512]{1,0:T(8,128)(2,1)S(1)} copy-done((bf16[128,512]{1,0:T(8,128)(2,1)S(1)}, bf16[128,512]{1,0:T(8,128)(2,1)}, u32[]{:S(2)}) %copy-start.3) | copy-done | bytes 131096
  5.1 0.0 copy-start.4
  5.1 0.9 %copy-done.4 = bf16[128,512]{1,0:T(8,128)(2,1)S(1)} copy-done((bf16[128,512]{1,0:T(8,128)(2,1)S(1)}, bf16[128,512]{1,0:T(8,128)(2,1)}, u32[]{:S(2)}) %copy-start.4) | copy-done | bytes 131096
  6.0 0.9 %copy-done.5 = bf16[128,512]{1,0:T(8,128)(2,1)S(1)} copy-done((bf16[128,512]{1,0:T(8,128)(2,1)S(1)}, bf16[128,512]{1,0:T(8,128)(2,1)}, u32[]{:S(2)}) %copy-start.5) | copy-done | bytes 131096
  6.9 69.6 %shard_map.152 = (bf16[128,512]{1,0:T(8,128)(2,1)S(1)}, bf16[128,512]{1,0:T(8,128)(2,1)S(1)}, bf16[128,512]{1,0:T(8,128)(2,1)S(1)}, bf16[128,512]{1,0:T(8,128)(2...) custom-call(bf16[128,512]{1,0:T(8,128)(2,1)S(1)} %copy-done, ...), custom_call_target="tpu_custom_call" | custom-call | tf_op jit(solution)/shard_map/pallas_call | solution.py:541
  76.5 0.7 copy.26
  77.1 0.7 copy.27
  77.8 0.7 copy.28
  78.4 0.7 copy.29
  79.1 0.7 copy.30
  79.8 0.7 copy.31
  80.4 0.6 copy.32
  81.0 0.6 copy.33
  (2 shorter events, 0.0 us)
Async XLA Ops:
  0.6 0.8 %copy-start.7 = (bf16[128,128]{1,0:T(8,128)(2,1)S(1)}, bf16[128,128]{1,0:T(8,128)(2,1)}, u32[]{:S(2)}) copy-start(bf16[128,128]{1,0:T(8,128)(2,1)} %v_s.1) | copy-start | bytes 98308
  0.6 0.8 copy-start.6
  1.5 0.9 %copy-start = (bf16[128,512]{1,0:T(8,128)(2,1)S(1)}, bf16[128,512]{1,0:T(8,128)(2,1)}, u32[]{:S(2)}) copy-start(bf16[128,512]{1,0:T(8,128)(2,1)} %q_l.1) | copy-start | bytes 393220
  2.4 0.9 %copy-start.1 = (bf16[128,512]{1,0:T(8,128)(2,1)S(1)}, bf16[128,512]{1,0:T(8,128)(2,1)}, u32[]{:S(2)}) copy-start(bf16[128,512]{1,0:T(8,128)(2,1)} %k_l.1) | copy-start | bytes 393220
  3.3 0.9 %copy-start.2 = (bf16[128,512]{1,0:T(8,128)(2,1)S(1)}, bf16[128,512]{1,0:T(8,128)(2,1)}, u32[]{:S(2)}) copy-start(bf16[128,512]{1,0:T(8,128)(2,1)} %v_l.1) | copy-start | bytes 393220
  4.2 0.9 %copy-start.3 = (bf16[128,512]{1,0:T(8,128)(2,1)S(1)}, bf16[128,512]{1,0:T(8,128)(2,1)}, u32[]{:S(2)}) copy-start(bf16[128,512]{1,0:T(8,128)(2,1)} %g_l.1) | copy-start | bytes 393220
  5.1 0.9 %copy-start.4 = (bf16[128,512]{1,0:T(8,128)(2,1)S(1)}, bf16[128,512]{1,0:T(8,128)(2,1)}, u32[]{:S(2)}) copy-start(bf16[128,512]{1,0:T(8,128)(2,1)} %q_s.1) | copy-start | bytes 393220
  6.0 0.9 %copy-start.5 = (bf16[128,512]{1,0:T(8,128)(2,1)S(1)}, bf16[128,512]{1,0:T(8,128)(2,1)}, u32[]{:S(2)}) copy-start(bf16[128,512]{1,0:T(8,128)(2,1)} %g_s.1) | copy-start | bytes 393220

commit v2 on v1

v2 whole, which is shorter than its diff:
```python
import jax
import jax.numpy as jnp
from jax import lax
from jax.experimental import pallas as pl
from jax.experimental.pallas import tpu as pltpu
from jax.sharding import PartitionSpec as P

DH = 128
ROWS = 128
NX = 4
NY = 8
HEADS = 4
WIDE = HEADS * DH
SPAN = NX * ROWS
CHUNK = 64
SCALE = DH**-0.5
LOG2E = 1.4426950408889634
MASKED = -1e30
F32 = jnp.float32
BF16 = jnp.bfloat16


def mm(a, b):
    return jnp.dot(a, b, preferred_element_type=F32)


def mm_nt(a, b):
    return lax.dot_general(a, b, (((1,), (1,)), ((), ())), preferred_element_type=F32)


def mm_tn(a, b):
    return lax.dot_general(a, b, (((0,), (0,)), ((), ())), preferred_element_type=F32)


def push(src, dst, send, recv, target):
    return pltpu.make_async_remote_copy(
        src_ref=src,
        dst_ref=dst,
        send_sem=send,
        recv_sem=recv,
        device_id={"ctx": target},
        device_id_type=pl.DeviceIdType.MESH,
    )


def split_log(total):
    high = total.astype(BF16)
    rest = total - high.astype(F32)
    middle = rest.astype(BF16)
    low = (rest - middle.astype(F32)).astype(BF16)
    return high, middle, low


def join_log(ref, first):
    return (
        ref[first : first + 16, :].astype(F32)
        + ref[first + 16 : first + 32, :].astype(F32)
        + ref[first + 32 : first + 48, :].astype(F32)
    )[0:1, :]


def kernel(
    q_hbm, k_hbm, v_hbm, g_hbm, ld_hbm, qs_hbm, ks_hbm, vs_hbm, gs_hbm,
    o_hbm, dq_hbm, dk_hbm, dv_hbm, os_hbm, dqs_hbm, dks_hbm, dvs_hbm,
    o_l, dq_l, dk_l, dv_l, o_s, dq_s, dk_s, dv_s,
    q_l, k_l, v_l, g_l, ld, qs, gs, qs_t, gs_t,
    kg, vg, e_ref, dp_ref, stat_m, stat_l, stat_t, dot_ref, wb_ref, ds_ref,
    out_t, dq_t, dkf, dkp, rbuf, dvp, vr, vsum, vfin, kfin, dks,
    lrow, lall, intra, lmsg, lin, ymsg, yin, cp, cg, lout, fin,
    in_s, out_s, kx_s, kx_r, kr_s, kr_r, vy_s, vy_r, vx_s, vx_r,
    l1_s, l1_r, y_s, y_r, l3_s, l3_r,
    dr_s, dr_r, du_s, du_r, dw_s, dw_r, kf_s, kf_r,
):
    me = lax.axis_index("ctx")
    y = lax.div(me, NX)
    x = lax.rem(me, NX)
    sigma = 1 - 2 * lax.rem(lax.axis_index("tp"), 2)

    def ring(value):
        return lax.rem(value + 2 * NY, NY)

    def at(yy, xx):
        return yy * NX + xx

    def col(step):
        return lax.rem(x + step + NX, NX)

    def when(condition):
        return pl.when(condition)

    barrier = pltpu.get_barrier_semaphore()
    for dx in range(1, NX):
        pl.semaphore_signal(
            barrier, inc=1, device_id={"ctx": at(y, col(dx))},
            device_id_type=pl.DeviceIdType.MESH,
        )
    for dy in range(1, NY):
        pl.semaphore_signal(
            barrier, inc=1, device_id={"ctx": at(ring(y + dy), x)},
            device_id_type=pl.DeviceIdType.MESH,
        )

    parts = [slice(h * DH, (h + 1) * DH) for h in range(HEADS)]
    moves = [(ks_hbm, kg.at[y, x]), (vs_hbm, vg.at[y, x]), (ld_hbm, ld)]
    moves += [(qs_hbm.at[:, part], qs.at[part, :]) for part in parts]
    moves += [(gs_hbm.at[:, part], gs.at[part, :]) for part in parts]
    moves += [(q_hbm, q_l), (k_hbm, k_l), (v_hbm, v_l), (g_hbm, g_l)]
    fetches = [
        pltpu.make_async_copy(src, dst, in_s.at[n]) for n, (src, dst) in enumerate(moves)
    ]
    for fetch in fetches:
        fetch.start()

    for r in range(NY):
        stat_m[r] = jnp.full((8, WIDE), MASKED, F32)
        stat_l[r] = jnp.zeros((8, WIDE), F32)
        stat_t[r] = jnp.zeros((8, WIDE), F32)
    out_t[...] = jnp.zeros_like(out_t)
    dq_t[...] = jnp.zeros_like(dq_t)
    cp[...] = jnp.zeros_like(cp)
    cg[...] = jnp.zeros_like(cg)
    for fetch in fetches[:3]:
        fetch.wait()
    pl.semaphore_wait(barrier, NX + NY - 2)

    def key_across(dx, owner):
        return push(
            kg.at[y, owner], kg.at[y, owner], kx_s.at[dx - 1], kx_r.at[dx - 1], at(y, col(dx))
        )

    def value_along(dy, owner):
        return push(
            vg.at[owner, x], vg.at[owner, x], vy_s.at[dy - 1], vy_r.at[dy - 1],
            at(ring(y + dy), x),
        )

    def value_across(dy, dx, row, owner):
        return push(
            vg.at[row, owner], vg.at[row, owner], vx_s.at[dy, dx - 1], vx_r.at[dy, dx - 1],
            at(y, col(dx)),
        )

    def key_ring(place, row, j, turn):
        block = kg.at[row, col(-j)]
        return push(
            block, block, kr_s.at[place - 1, j], kr_r.at[place - 1, j], at(ring(y + turn), x)
        )

    def wanted(row, turn, target, far):
        return jnp.where(turn > 0, row < target, row < far)

    def key_start(place, row, j, turn, far):
        @when(wanted(row, turn, ring(y + turn), far))
        def _():
            key_ring(place, row, j, turn).start()

    for dx in range(1, NX):
        key_across(dx, x).start()
    key_start(1, y, 0, sigma, 4)
    key_start(2, y, 0, -sigma, 3)
    for dy in (1, 7, 2, 6, 3, 5, 4):
        @when(y + dy < NY)
        def _():
            value_along(dy, y).start()
    for dx in range(1, NX):
        value_across(0, dx, y, x).start()

    def block_scores(row, b, masked):
        scores = mm(kg[row, b], qs_t[...])
        if masked:
            key_at = lax.broadcasted_iota(jnp.int32, (ROWS, WIDE), 0) + b * ROWS
            query_at = lax.rem(lax.broadcasted_iota(jnp.int32, (ROWS, WIDE), 1), ROWS)
            scores = jnp.where(key_at <= query_at + x * ROWS, scores, MASKED)
        e_ref[row, pl.ds(pl.multiple_of(b * ROWS, ROWS), ROWS), :] = scores
        top = jnp.max(scores.reshape(ROWS // 8, 8, WIDE), axis=0)
        stat_m[row] = jnp.maximum(stat_m[row], top)

    def row_weights(row):
        top = jnp.max(stat_m[row], axis=0, keepdims=True)
        stat_m[row] = jnp.broadcast_to(top, (8, WIDE))
        shift = top * (SCALE * LOG2E)

        def turn(i, total):
            rows = pl.ds(pl.multiple_of(i * CHUNK, CHUNK), CHUNK)
            grown = jnp.exp2(e_ref[row, rows, :] * (SCALE * LOG2E) - shift)
            e_ref[row, rows, :] = grown
            return total + jnp.sum(grown.reshape(CHUNK // 8, 8, WIDE), axis=0)

        total = lax.fori_loop(0, SPAN // CHUNK, turn, jnp.zeros((8, WIDE), F32))
        stat_l[row] = jnp.broadcast_to(jnp.sum(total, axis=0, keepdims=True), (8, WIDE))

    def light_send(h, owner):
        return push(lmsg.at[h], lin.at[owner], l1_s.at[h], l1_r.at[owner], at(y, h))

    def light_head(h):
        cols = pl.ds(pl.multiple_of(h * DH, DH), DH)
        qh, kh, vh, gh = q_l[:, cols], k_l[:, cols], v_l[:, cols], g_l[:, cols]
        flat = jnp.broadcast_to(lrow[pl.ds(h, 1), :], (ROWS, ROWS))
        level = flat.T
        lall[:, cols] = level
        row_at = lax.broadcasted_iota(jnp.int32, (ROWS, ROWS), 0)
        causal = row_at >= lax.broadcasted_iota(jnp.int32, (ROWS, ROWS), 1)
        gaps = jnp.where(causal, level - flat, 0.0)
        weights = jnp.where(causal, jnp.exp(gaps), 0.0) * SCALE
        mixing = (mm_nt(qh, kh) * weights).astype(BF16)
        back_mix = (mm_nt(gh, vh) * weights).astype(BF16)
        intra[0, :, cols] = mm(mixing, vh)
        intra[1, :, cols] = mm(back_mix, kh)
        intra[2, :, cols] = mm_tn(back_mix, qh)
        intra[3, :, cols] = mm_tn(mixing, gh)
        last = level[ROWS - 1 : ROWS, :]
        fading = (kh.astype(F32) * jnp.exp(last - level)).astype(BF16)
        entering = (qh.astype(F32) * jnp.exp(level)).astype(BF16)
        lmsg[h, 0:DH, :] = mm_tn(fading, vh).astype(BF16)
        lmsg[h, DH : 2 * DH, :] = mm_tn(entering, gh).astype(BF16)
        for n, term in enumerate(split_log(jnp.broadcast_to(last, (16, DH)))):
            lmsg[h, 2 * DH + 16 * n : 2 * DH + 16 * (n + 1), :] = term

        @when(h != x)
        def _():
            light_send(h, x).start()

        @when(h == x)
        def _():
            lin[x] = lmsg[h]

    upper = (
        lax.broadcasted_iota(jnp.int32, (ROWS, ROWS), 0)
        <= lax.broadcasted_iota(jnp.int32, (ROWS, ROWS), 1)
    ).astype(F32)
    lrow[...] = jnp.dot(
        ld[...], upper, precision=lax.Precision.HIGHEST, preferred_element_type=F32
    )
    for fetch in fetches[3:]:
        fetch.wait()
    for part in parts:
        qs_t[:, part] = qs[part, :].T
        gs_t[:, part] = gs[part, :].T

    block_scores(y, x, True)
    for j in range(1, NX):
        key_across(j, col(-j)).wait_recv()
        key_start(1, y, j, sigma, 4)
        key_start(2, y, j, -sigma, 3)
        block_scores(y, col(-j), True)
    light_head(0)
    row_weights(y)
    light_head(1)

    def key_take(place, row, j, turn, far, last):
        @when(wanted(row, turn, y, far))
        def _():
            key_ring(place, row, j, turn).wait_recv()

            @when(jnp.logical_not(last))
            def _():
                key_start(place + 2, row, j, turn, far)

            @when(row < y)
            def _():
                block_scores(row, col(-j), False)

    def value_pass(dy):
        @when(y >= dy)
        def _():
            value_along(dy, ring(y - dy)).wait_recv()
            for dx in range(1, NX):
                value_across(dy, dx, ring(y - dy), x).start()

    def value_take(dy):
        @when(y >= dy)
        def _():
            row = ring(y - dy)
            for dx in range(1, NX):
                value_across(dy, dx, row, col(-dx)).wait_recv()
            total = jnp.zeros((8, WIDE), F32)
            for b in range(NX):
                grads = mm(vg[row, b], gs_t[...])
                dp_ref[row, b * ROWS : (b + 1) * ROWS, :] = grads
                weighed = grads * e_ref[row, b * ROWS : (b + 1) * ROWS, :]
                total = total + jnp.sum(weighed.reshape(ROWS // 8, 8, WIDE), axis=0)
            stat_t[row] = jnp.broadcast_to(jnp.sum(total, axis=0, keepdims=True), (8, WIDE))

    def gather_turn(k, _):
        row_a = ring(y - sigma * k)
        row_b = ring(y + sigma * k)

        def block_turn(j, _):
            key_take(2 * k - 1, row_a, j, sigma, 4, k < 0)
            key_take(2 * k, row_b, j, -sigma, 3, k == 3)
            return 0

        lax.fori_loop(0, NX, block_turn, 0)
        value_pass(k)
        value_pass(NY - k)

        @when(row_a < y)
        def _():
            row_weights(row_a)

        @when(row_b < y)
        def _():
            row_weights(row_b)

        @when(k < 3)
        def _():
            light_head(k + 1)

        value_take(k - 1)

        @when(k > 1)
        def _():
            value_take(NY + 1 - k)

        return 0

    lax.fori_loop(1, NY // 2, gather_turn, 0)
    value_pass(NY // 2)
    row_far = ring(y - sigma * (NY // 2))

    def far_turn(j, _):
        key_take(NY - 1, row_far, j, sigma, 4, j >= 0)
        return 0

    lax.fori_loop(0, NX, far_turn, 0)

    @when(row_far < y)
    def _():
        row_weights(row_far)

    for h in range(NX):
        @when(h != x)
        def _():
            push(lmsg.at[h], lin.at[h], l1_s.at[h], l1_r.at[h], at(y, h)).wait_recv()
    levels = [join_log(lin.at[b], 2 * DH) for b in range(NX)]
    row_state = lin[0, 0:DH, :].astype(F32)
    for b in range(1, NX):
        row_state = jnp.exp(levels[b]) * row_state + lin[b, 0:DH, :].astype(F32)
    row_grad = lin[NX - 1, DH : 2 * DH, :].astype(F32)
    for b in range(NX - 2, -1, -1):
        row_grad = jnp.exp(levels[b]) * row_grad + lin[b, DH : 2 * DH, :].astype(F32)
    row_level = jnp.broadcast_to(levels[0] + levels[1] + levels[2] + levels[3], (16, DH))
    ymsg[0, 0:DH, :] = row_state.astype(BF16)
    ymsg[1, 0:DH, :] = row_grad.astype(BF16)
    for n, term in enumerate(split_log(row_level)):
        ymsg[0, DH + 16 * n : DH + 16 * (n + 1), :] = term
        ymsg[1, DH + 16 * n : DH + 16 * (n + 1), :] = term

    def state_along(dy, owner):
        kind = jnp.where(y + dy < NY, 0, 1)
        return push(
            ymsg.at[kind], yin.at[owner], y_s.at[dy - 1], y_r.at[dy - 1], at(ring(y + dy), x)
        )

    for dy in range(1, NY):
        state_along(dy, y).start()

    value_take(NY // 2 - 1)
    value_take(NY // 2 + 1)
    value_take(NY // 2)

    top = stat_m[0]
    for r in range(1, NY):
        top = jnp.maximum(top, stat_m[r])
    total = jnp.zeros((8, WIDE), F32)
    dots = jnp.zeros((8, WIDE), F32)
    for r in range(NY):
        factor = jnp.exp2((stat_m[r] - top) * (SCALE * LOG2E))
        total = total + factor * stat_l[r]
        dots = dots + factor * stat_t[r]
        stat_m[r] = factor
    inverse = 1.0 / total
    dot_ref[...] = dots * inverse
    for r in range(NY):
        stat_l[r] = stat_m[r] * inverse

    def state_back(b, owner):
        return push(lout.at[b], fin.at[owner], l3_s.at[b], l3_r.at[owner], at(y, b))

    def state_turn():
        for dy in range(1, NY):
            state_along(dy, ring(y - dy)).wait_recv()
        for yy in range(NY):
            @when(yy < y)
            def _():
                cp[...] = (
                    jnp.exp(join_log(yin.at[yy], DH)) * cp[...] + yin[yy, 0:DH, :].astype(F32)
                )
        for yy in range(NY - 1, -1, -1):
            @when(yy > y)
            def _():
                cg[...] = (
                    jnp.exp(join_log(yin.at[yy], DH)) * cg[...] + yin[yy, 0:DH, :].astype(F32)
                )
        factors = [jnp.exp(join_log(lin.at[b], 2 * DH)) for b in range(NX)]
        carried = cp[...]
        for b in range(NX):
            lout[b, 0:DH, :] = carried.astype(BF16)
            carried = factors[b] * carried + lin[b, 0:DH, :].astype(F32)
        carried = cg[...]
        for b in range(NX - 1, -1, -1):
            lout[b, DH : 2 * DH, :] = carried.astype(BF16)
            carried = factors[b] * carried + lin[b, DH : 2 * DH, :].astype(F32)
        for b in range(NX):
            @when(b != x)
            def _():
                state_back(b, x).start()
        fin[x] = lout[x]

    def grad_ring(place, b, turn):
        return push(
            dkp.at[place, b], rbuf.at[place, b], dr_s.at[place, b], dr_r.at[place, b],
            at(ring(y + turn), x),
        )

    def grad_sent(row, turn, sender, far):
        return jnp.where(turn < 0, row < sender, row < far)

    def dv_across(row, dx):
        return push(
            dvp.at[row, col(dx)], vr.at[row, dx - 1], du_s.at[row, dx - 1], du_r.at[row, dx - 1],
            at(y, col(dx)),
        )

    def dv_along(row, owner):
        return push(vsum.at[row], vfin.at[owner], dw_s.at[row], dw_r.at[owner], at(row, x))

    def dv_sum(row):
        for dx in range(1, NX):
            dv_across(row, dx).wait_recv()
        return (
            dvp[row, x].astype(F32)
            + vr[row, 0].astype(F32)
            + vr[row, 1].astype(F32)
            + vr[row, 2].astype(F32)
        )

    def place_row(place):
        forth = (lax.rem(place, 2) == 1) | (place == 0)
        turn = jnp.where(forth, sigma, -sigma)
        far = jnp.where(forth, 4, 3)
        return turn, far, ring(y + turn * (4 - lax.div(place + 1, 2)))

    def back_turn(place, _):
        turn, far, row = place_row(place)

        @when(row <= y)
        def _():
            def weigh(i, _):
                rows = pl.ds(pl.multiple_of(i * CHUNK, CHUNK), CHUNK)
                weights = e_ref[row, rows, :] * stat_l[row, 0:1, :]
                wb_ref[rows, :] = weights.astype(BF16)
                ds_ref[rows, :] = (weights * (dp_ref[row, rows, :] - dot_ref[0:1, :])).astype(BF16)
                return 0

            lax.fori_loop(0, SPAN // CHUNK, weigh, 0)
            dkf[...] = (mm(ds_ref[...], qs[...]) * SCALE).reshape(NX, ROWS, DH)
            dvp[row] = mm(wb_ref[...], gs[...]).astype(BF16).reshape(NX, ROWS, DH)
            for dx in range(1, NX):
                dv_across(row, dx).start()

        @when(row > y)
        def _():
            dkf[...] = jnp.zeros_like(dkf)

        before = jnp.where(place == 1, 0, jnp.maximum(place - 2, 0))
        takes = (place != 0) & (place != 2) & (place != NY - 1)
        takes = takes & grad_sent(row, turn, ring(y - turn), far)
        sends = (place < NY - 1) & grad_sent(row, turn, y, far)

        def ring_block(b, _):
            @when(takes)
            def _():
                grad_ring(before, b, turn).wait_recv()
                dkf[b] += rbuf[before, b].astype(F32)

            @when(sends)
            def _():
                dkp[place, b] = dkf[b].astype(BF16)
                grad_ring(place, b, turn).start()

            return 0

        lax.fori_loop(0, NX, ring_block, 0)

        @when(row <= y)
        def _():
            out_t[...] += mm_tn(vg[row].reshape(SPAN, DH), wb_ref[...])
            dq_t[...] += mm_tn(kg[row].reshape(SPAN, DH), ds_ref[...])

        @when(place >= 1)
        def _():
            _, _, before_row = place_row(place - 1)

            @when(before_row < y)
            def _():
                vsum[before_row] = dv_sum(before_row).astype(BF16)
                dv_along(before_row, y).start()

        @when(place == 2)
        def _():
            state_turn()

        return 0

    lax.fori_loop(0, NY, back_turn, 0)

    for b in range(NX):
        @when(b != x)
        def _():
            push(lout.at[b], fin.at[b], l3_s.at[b], l3_r.at[b], at(y, b)).wait_recv()

    def light_out(h, _):
        cols = pl.ds(pl.multiple_of(h * DH, DH), DH)
        qh, kh, vh, gh = q_l[:, cols], k_l[:, cols], v_l[:, cols], g_l[:, cols]
        level = lall[:, cols]
        entering = jnp.exp(level) * SCALE
        fading = jnp.exp(level[ROWS - 1 : ROWS, :] - level) * SCALE
        prior = fin[h, 0:DH, :]
        later = fin[h, DH : 2 * DH, :]
        o_l[:, cols] = (intra[0, :, cols] + entering * mm(qh, prior)).astype(BF16)
        dq_l[:, cols] = (intra[1, :, cols] + entering * mm_nt(gh, prior)).astype(BF16)
        dk_l[:, cols] = (intra[2, :, cols] + fading * mm_nt(vh, later)).astype(BF16)
        dv_l[:, cols] = (intra[3, :, cols] + fading * mm(kh, later)).astype(BF16)
        return 0

    lax.fori_loop(0, HEADS, light_out, 0)
    moves = [(o_l, o_hbm), (dq_l, dq_hbm), (dk_l, dk_hbm), (dv_l, dv_hbm)]
    moves += [(o_s, os_hbm), (dq_s, dqs_hbm), (dk_s, dks_hbm), (dv_s, dvs_hbm)]
    stores = [
        pltpu.make_async_copy(src, dst, out_s.at[n]) for n, (src, dst) in enumerate(moves)
    ]
    for store in stores[:4]:
        store.start()

    def dk_across(dx):
        return push(
            dks.at[col(dx)], kfin.at[dx - 1], kf_s.at[dx - 1], kf_r.at[dx - 1], at(y, col(dx))
        )

    for j in (1, 2, 3, 0):
        b = col(j)
        for place, turn, far in ((NY - 3, sigma, 4), (NY - 2, -sigma, 3)):
            @when(grad_sent(y, turn, ring(y - turn), far))
            def _():
                grad_ring(place, b, turn).wait_recv()
                dkf[b] += rbuf[place, b].astype(F32)
        if j:
            dks[b] = dkf[b].astype(BF16)
            dk_across(j).start()

    for part in parts:
        o_s[:, part] = out_t[:, part].T.astype(BF16)
        dq_s[:, part] = (dq_t[:, part].T * SCALE).astype(BF16)
    stores[4].start()
    stores[5].start()

    cp[...] = dv_sum(y)
    for yy in range(1, NY):
        @when(yy > y)
        def _():
            push(vsum.at[yy], vfin.at[yy], dw_s.at[yy], dw_r.at[yy], at(yy, x)).wait_recv()
            cp[...] += vfin[yy].astype(F32)
    dv_s[...] = cp[...].astype(BF16)
    stores[7].start()

    for dx in range(1, NX):
        dk_across(dx).wait_recv()
    dk_s[...] = (
        dkf[x] + kfin[0].astype(F32) + kfin[1].astype(F32) + kfin[2].astype(F32)
    ).astype(BF16)
    stores[6].start()

    for dx in range(1, NX):
        key_across(dx, x).wait_send()
        dk_across(dx).wait_send()

    def sent_turn(place, _):
        odd = lax.rem(place, 2) == 1
        turn = jnp.where(odd, sigma, -sigma)
        row = ring(y - turn * (lax.div(place + 1, 2) - 1))

        @when(wanted(row, turn, ring(y + turn), jnp.where(odd, 4, 3)))
        def _():
            for j in range(NX):
                key_ring(place, row, j, turn).wait_send()

        turn_back, far_back, row_back = place_row(place - 1)

        @when(grad_sent(row_back, turn_back, y, far_back))
        def _():
            for j in range(NX):
                grad_ring(place - 1, j, turn_back).wait_send()

        return 0

    lax.fori_loop(1, NY, sent_turn, 0)
    for dy in range(1, NY):
        state_along(dy, y).wait_send()

        @when(y + dy < NY)
        def _():
            value_along(dy, y).wait_send()

        @when(dy - 1 < y)
        def _():
            dv_along(dy - 1, y).wait_send()
    for b in range(NX):
        @when(b != x)
        def _():
            light_send(b, x).wait_send()
            state_back(b, x).wait_send()
    for dy in range(NY):
        @when(dy <= y)
        def _():
            for dx in range(1, NX):
                value_across(dy, dx, ring(y - dy), x).wait_send()
                dv_across(dy, dx).wait_send()
    for store in stores:
        store.wait()


def copy_out(*refs):
    ins, outs, sems = refs[:8], refs[8:16], refs[16]
    copies = [pltpu.make_async_copy(a, b, sems.at[n]) for n, (a, b) in enumerate(zip(ins, outs))]
    for copy in copies:
        copy.start()
    for copy in copies:
        copy.wait()


def shards(q_light, k_light, v_light, g_light, log_decay, q_soft, k_soft, v_soft, g_soft):
    dma = pltpu.SemaphoreType.DMA
    wide = jax.ShapeDtypeStruct((ROWS, WIDE), BF16)
    narrow = jax.ShapeDtypeStruct((ROWS, DH), BF16)
    scratch = [pltpu.VMEM((ROWS, WIDE), BF16)] * 6 + [pltpu.VMEM((ROWS, DH), BF16)] * 2
    scratch += [
        pltpu.VMEM((ROWS, WIDE), BF16),
        pltpu.VMEM((ROWS, WIDE), BF16),
        pltpu.VMEM((ROWS, WIDE), BF16),
        pltpu.VMEM((ROWS, WIDE), BF16),
        pltpu.VMEM((HEADS, ROWS), F32),
        pltpu.VMEM((WIDE, DH), BF16),
        pltpu.VMEM((WIDE, DH), BF16),
        pltpu.VMEM((DH, WIDE), BF16),
        pltpu.VMEM((DH, WIDE), BF16),
        pltpu.VMEM((NY, NX, ROWS, DH), BF16),
        pltpu.VMEM((NY, NX, ROWS, DH), BF16),
        pltpu.VMEM((NY, SPAN, WIDE), F32),
        pltpu.VMEM((NY, SPAN, WIDE), F32),
        pltpu.VMEM((NY, 8, WIDE), F32),
        pltpu.VMEM((NY, 8, WIDE), F32),
        pltpu.VMEM((NY, 8, WIDE), F32),
        pltpu.VMEM((8, WIDE), F32),
        pltpu.VMEM((SPAN, WIDE), BF16),
        pltpu.VMEM((SPAN, WIDE), BF16),
        pltpu.VMEM((DH, WIDE), F32),
        pltpu.VMEM((DH, WIDE), F32),
        pltpu.VMEM((NX, ROWS, DH), F32),
        pltpu.VMEM((NY - 1, NX, ROWS, DH), BF16),
        pltpu.VMEM((NY - 1, NX, ROWS, DH), BF16),
        pltpu.VMEM((NY, NX, ROWS, DH), BF16),
        pltpu.VMEM((NY, NX - 1, ROWS, DH), BF16),
        pltpu.VMEM((NY, ROWS, DH), BF16),
        pltpu.VMEM((NY, ROWS, DH), BF16),
        pltpu.VMEM((NX - 1, ROWS, DH), BF16),
        pltpu.VMEM((NX, ROWS, DH), BF16),
        pltpu.VMEM((HEADS, ROWS), F32),
        pltpu.VMEM((ROWS, WIDE), F32),
        pltpu.VMEM((4, ROWS, WIDE), F32),
        pltpu.VMEM((HEADS, 2 * DH + 48, DH), BF16),
        pltpu.VMEM((NX, 2 * DH + 48, DH), BF16),
        pltpu.VMEM((2, DH + 48, DH), BF16),
        pltpu.VMEM((NY, DH + 48, DH), BF16),
        pltpu.VMEM((DH, DH), F32),
        pltpu.VMEM((DH, DH), F32),
        pltpu.VMEM((NX, 2 * DH, DH), BF16),
        pltpu.VMEM((HEADS, 2 * DH, DH), BF16),
        dma((15,)),
        dma((8,)),
        dma((NX - 1,)), dma((NX - 1,)),
        dma((NY - 1, NX)), dma((NY - 1, NX)),
        dma((NY - 1,)), dma((NY - 1,)),
        dma((NY, NX - 1)), dma((NY, NX - 1)),
        dma((NX,)), dma((NX,)),
        dma((NY - 1,)), dma((NY - 1,)),
        dma((NX,)), dma((NX,)),
        dma((NY - 1, NX)), dma((NY - 1, NX)),
        dma((NY, NX - 1)), dma((NY, NX - 1)),
        dma((NY,)), dma((NY,)),
        dma((NX - 1,)), dma((NX - 1,)),
    ]
    hbm = pl.BlockSpec(memory_space=pltpu.HBM)
    room = 62 * 1024 * 1024
    shapes = (wide, wide, wide, wide, wide, wide, narrow, narrow)
    results = pl.pallas_call(
        kernel,
        out_shape=shapes,
        in_specs=[hbm] * 9,
        out_specs=(hbm,) * 8,
        scratch_shapes=scratch,
        compiler_params=pltpu.CompilerParams(
            collective_id=0, has_side_effects=True, vmem_limit_bytes=room
        ),
    )(q_light, k_light, v_light, g_light, log_decay.T, q_soft, k_soft, v_soft, g_soft)
    return pl.pallas_call(
        copy_out,
        out_shape=shapes,
        in_specs=[hbm] * 8,
        out_specs=(hbm,) * 8,
        scratch_shapes=[dma((8,))],
        compiler_params=pltpu.CompilerParams(vmem_limit_bytes=room),
    )(*results)


def solution(mesh):
    spec = P(("dp", "ctx"), "tp")
    return jax.shard_map(
        shards, mesh=mesh, in_specs=(spec,) * 9, out_specs=(spec,) * 8, check_vma=False
    )
```

time: 81.9 us -> 92.9 us (1.13)
  the two profiles are of different devices: /device:TPU:392 before, /device:TPU:256 now
where the time goes in v2:
time: 92.9 us; the launch traced here: 92.7 us
  Pallas kernels  92.1 us (99%)
    pallas_call x1, Pallas kernels, shards(): pl.pallas_call(kernel, out_shape=shapes, in_specs=[hbm] * 9, out_specs=(h...  65.1 us
    pallas_call x1, Pallas kernels, shards(): pl.pallas_call(copy_out, out_shape=shapes, in_specs=[hbm] * 8, out_specs=...  27 us

profile of v2, /device:TPU:256, one launch (start us, length us, event | category | flops | bytes accessed | tf_op | source)
XLA Modules:
  0.0 92.7 jit_solution(15052415083573235973)
XLA Ops:
  0.6 65.1 %shard_map.152 = (bf16[128,512]{1,0:T(8,128)(2,1)}, bf16[128,512]{1,0:T(8,128)(2,1)}, bf16[128,512]{1,0:T(8,128)(2,1)}, bf16[128,512]{1,0:T(8,128)(2,1)}, bf16[1...) custom-call(bf16[128,512]{1,0:T(8,128)(2,1)} %q_hbm.1, ...), custom_call_target="tpu_custom_call" | custom-call | tf_op jit(solution)/shard_map/pallas_call | solution.py:696
  65.7 27.0 %shard_map.153 = (bf16[128,512]{1,0:T(8,128)(2,1)}, bf16[128,512]{1,0:T(8,128)(2,1)}, bf16[128,512]{1,0:T(8,128)(2,1)}, bf16[128,512]{1,0:T(8,128)(2,1)}, bf16[1...) custom-call(bf16[128,512]{1,0:T(8,128)(2,1)} %get-tuple-element.16.refs_0_, ...), custom_call_target="tpu_custom_call" | custom-call | tf_op jit(solution)/shard_map/pallas_call | solution.py:706

commit v3 on v2

--- a/solution.py
+++ b/solution.py
@@ -12,7 +12,6 @@
 HEADS = 4
 WIDE = HEADS * DH
 SPAN = NX * ROWS
-CHUNK = 64
 SCALE = DH**-0.5
 LOG2E = 1.4426950408889634
 MASKED = -1e30
@@ -65,9 +64,9 @@
     o_l, dq_l, dk_l, dv_l, o_s, dq_s, dk_s, dv_s,
     q_l, k_l, v_l, g_l, ld, qs, gs, qs_t, gs_t,
     kg, vg, e_ref, dp_ref, stat_m, stat_l, stat_t, dot_ref, wb_ref, ds_ref,
-    out_t, dq_t, dkf, dkp, rbuf, dvp, vr, vsum, vfin, kfin, dks,
+    out_t, dq_t, dkf, dkp, rbuf, dvp, vr, vsum, vfin, vacc, kfin, dks,
     lrow, lall, intra, lmsg, lin, ymsg, yin, cp, cg, lout, fin,
-    in_s, out_s, kx_s, kx_r, kr_s, kr_r, vy_s, vy_r, vx_s, vx_r,
+    in_s, out_s, kx_s, kx_r, kr_s, kr_r, vx_s, vx_r,
     l1_s, l1_r, y_s, y_r, l3_s, l3_r,
     dr_s, dr_r, du_s, du_r, dw_s, dw_r, kf_s, kf_r,
 ):
@@ -111,10 +110,10 @@
     for fetch in fetches:
         fetch.start()
 
-    for r in range(NY):
-        stat_m[r] = jnp.full((8, WIDE), MASKED, F32)
-        stat_l[r] = jnp.zeros((8, WIDE), F32)
-        stat_t[r] = jnp.zeros((8, WIDE), F32)
+    halves = [slice(0, WIDE // 2), slice(WIDE // 2, WIDE)]
+    stat_m[...] = jnp.full(stat_m.shape, MASKED, F32)
+    stat_l[...] = jnp.zeros_like(stat_l)
+    stat_t[...] = jnp.zeros_like(stat_t)
     out_t[...] = jnp.zeros_like(out_t)
     dq_t[...] = jnp.zeros_like(dq_t)
     cp[...] = jnp.zeros_like(cp)
@@ -128,20 +127,15 @@
             kg.at[y, owner], kg.at[y, owner], kx_s.at[dx - 1], kx_r.at[dx - 1], at(y, col(dx))
         )
 
-    def value_along(dy, owner):
+    def value_across(row, i, owner):
         return push(
-            vg.at[owner, x], vg.at[owner, x], vy_s.at[dy - 1], vy_r.at[dy - 1],
-            at(ring(y + dy), x),
-        )
-
-    def value_across(dy, dx, row, owner):
-        return push(
-            vg.at[row, owner], vg.at[row, owner], vx_s.at[dy, dx - 1], vx_r.at[dy, dx - 1],
-            at(y, col(dx)),
+            vg.at[row, owner], vg.at[row, owner], vx_s.at[row, i], vx_r.at[row, i],
+            at(y, col(-sigma if i == 1 else sigma)),
         )
 
     def key_ring(place, row, j, turn):
-        block = kg.at[row, col(-j)]
+        values = isinstance(j, int) and j == NX
+        block = vg.at[row, x] if values else kg.at[row, col(-j)]
         return push(
             block, block, kr_s.at[place - 1, j], kr_r.at[place - 1, j], at(ring(y + turn), x)
         )
@@ -156,38 +150,26 @@
 
     for dx in range(1, NX):
         key_across(dx, x).start()
-    key_start(1, y, 0, sigma, 4)
-    key_start(2, y, 0, -sigma, 3)
-    for dy in (1, 7, 2, 6, 3, 5, 4):
-        @when(y + dy < NY)
-        def _():
-            value_along(dy, y).start()
-    for dx in range(1, NX):
-        value_across(0, dx, y, x).start()
-
-    def block_scores(row, b, masked):
-        scores = mm(kg[row, b], qs_t[...])
-        if masked:
-            key_at = lax.broadcasted_iota(jnp.int32, (ROWS, WIDE), 0) + b * ROWS
-            query_at = lax.rem(lax.broadcasted_iota(jnp.int32, (ROWS, WIDE), 1), ROWS)
-            scores = jnp.where(key_at <= query_at + x * ROWS, scores, MASKED)
-        e_ref[row, pl.ds(pl.multiple_of(b * ROWS, ROWS), ROWS), :] = scores
-        top = jnp.max(scores.reshape(ROWS // 8, 8, WIDE), axis=0)
-        stat_m[row] = jnp.maximum(stat_m[row], top)
-
-    def row_weights(row):
-        top = jnp.max(stat_m[row], axis=0, keepdims=True)
-        stat_m[row] = jnp.broadcast_to(top, (8, WIDE))
-        shift = top * (SCALE * LOG2E)
-
-        def turn(i, total):
-            rows = pl.ds(pl.multiple_of(i * CHUNK, CHUNK), CHUNK)
-            grown = jnp.exp2(e_ref[row, rows, :] * (SCALE * LOG2E) - shift)
-            e_ref[row, rows, :] = grown
-            return total + jnp.sum(grown.reshape(CHUNK // 8, 8, WIDE), axis=0)
-
-        total = lax.fori_loop(0, SPAN // CHUNK, turn, jnp.zeros((8, WIDE), F32))
-        stat_l[row] = jnp.broadcast_to(jnp.sum(total, axis=0, keepdims=True), (8, WIDE))
+    for j in (NX, 0):
+        key_start(1, y, j, sigma, 4)
+        key_start(2, y, j, -sigma, 3)
+    value_across(y, 0, x).start()
+    value_across(y, 1, x).start()
+
+    def row_scores(row, masked):
+        for b in range(NX):
+            rows = slice(b * ROWS, (b + 1) * ROWS)
+            for cols in halves:
+                scores = mm(kg[row, b], qs_t[:, cols])
+                if masked:
+                    key_at = lax.broadcasted_iota(jnp.int32, scores.shape, 0) + b * ROWS
+                    query_at = lax.rem(lax.broadcasted_iota(jnp.int32, scores.shape, 1), ROWS)
+                    scores = jnp.where(key_at <= query_at + x * ROWS, scores, MASKED)
+                top = jnp.max(scores, axis=0, keepdims=True)
+                grown = jnp.exp2(scores * (SCALE * LOG2E) - top * (SCALE * LOG2E))
+                e_ref[row, rows, cols] = grown
+                stat_m[pl.ds(row * NX + b, 1), cols] = top
+                stat_l[pl.ds(row * NX + b, 1), cols] = jnp.sum(grown, axis=0, keepdims=True)
 
     def light_send(h, owner):
         return push(lmsg.at[h], lin.at[owner], l1_s.at[h], l1_r.at[owner], at(y, h))
@@ -237,14 +219,12 @@
         qs_t[:, part] = qs[part, :].T
         gs_t[:, part] = gs[part, :].T
 
-    block_scores(y, x, True)
     for j in range(1, NX):
         key_across(j, col(-j)).wait_recv()
         key_start(1, y, j, sigma, 4)
         key_start(2, y, j, -sigma, 3)
-        block_scores(y, col(-j), True)
+    row_scores(y, True)
     light_head(0)
-    row_weights(y)
     light_head(1)
 
     def key_take(place, row, j, turn, far, last):
@@ -256,34 +236,41 @@
             def _():
                 key_start(place + 2, row, j, turn, far)
 
-            @when(row < y)
-            def _():
-                block_scores(row, col(-j), False)
-
-    def value_pass(dy):
-        @when(y >= dy)
-        def _():
-            value_along(dy, ring(y - dy)).wait_recv()
-            for dx in range(1, NX):
-                value_across(dy, dx, ring(y - dy), x).start()
-
-    def value_take(dy):
-        @when(y >= dy)
-        def _():
-            row = ring(y - dy)
-            for dx in range(1, NX):
-                value_across(dy, dx, row, col(-dx)).wait_recv()
-            total = jnp.zeros((8, WIDE), F32)
+    def value_pass(row):
+        @when(row < y)
+        def _():
+            value_across(row, 0, x).start()
+            value_across(row, 1, x).start()
+
+    def value_relay(row):
+        @when(row <= y)
+        def _():
+            value_across(row, 0, col(-sigma)).wait_recv()
+            value_across(row, 2, col(-sigma)).start()
+
+    def value_take(row):
+        @when(row <= y)
+        def _():
+            value_across(row, 1, col(sigma)).wait_recv()
+            value_across(row, 2, col(2)).wait_recv()
             for b in range(NX):
-                grads = mm(vg[row, b], gs_t[...])
-                dp_ref[row, b * ROWS : (b + 1) * ROWS, :] = grads
-                weighed = grads * e_ref[row, b * ROWS : (b + 1) * ROWS, :]
-                total = total + jnp.sum(weighed.reshape(ROWS // 8, 8, WIDE), axis=0)
-            stat_t[row] = jnp.broadcast_to(jnp.sum(total, axis=0, keepdims=True), (8, WIDE))
+                rows = slice(b * ROWS, (b + 1) * ROWS)
+                for cols in halves:
+                    grads = mm(vg[row, b], gs_t[:, cols])
+                    dp_ref[row, rows, cols] = grads
+                    weighed = jnp.sum(grads * e_ref[row, rows, cols], axis=0, keepdims=True)
+                    stat_t[pl.ds(row * NX + b, 1), cols] = weighed
+
+    def rows_at(k):
+        return ring(y - sigma * k), ring(y + sigma * k)
 
     def gather_turn(k, _):
-        row_a = ring(y - sigma * k)
-        row_b = ring(y + sigma * k)
+        row_a, row_b = rows_at(k)
+        past_a, past_b = rows_at(k - 1)
+        key_take(2 * k - 1, row_a, NX, sigma, 4, k < 0)
+        value_pass(row_a)
+        key_take(2 * k, row_b, NX, -sigma, 3, k == 3)
+        value_pass(row_b)
 
         def block_turn(j, _):
             key_take(2 * k - 1, row_a, j, sigma, 4, k < 0)
@@ -291,42 +278,51 @@
             return 0
 
         lax.fori_loop(0, NX, block_turn, 0)
-        value_pass(k)
-        value_pass(NY - k)
+        value_relay(past_a)
+
+        @when(k > 1)
+        def _():
+            value_relay(past_b)
 
         @when(row_a < y)
         def _():
-            row_weights(row_a)
+            row_scores(row_a, False)
 
         @when(row_b < y)
         def _():
-            row_weights(row_b)
+            row_scores(row_b, False)
 
         @when(k < 3)
         def _():
             light_head(k + 1)
 
-        value_take(k - 1)
+        value_take(past_a)
 
         @when(k > 1)
         def _():
-            value_take(NY + 1 - k)
+            value_take(past_b)
 
         return 0
 
     lax.fori_loop(1, NY // 2, gather_turn, 0)
-    value_pass(NY // 2)
+    past_a, past_b = rows_at(NY // 2 - 1)
     row_far = ring(y - sigma * (NY // 2))
+    key_take(NY - 1, row_far, NX, sigma, 4, row_far >= 0)
+    value_pass(row_far)
 
     def far_turn(j, _):
         key_take(NY - 1, row_far, j, sigma, 4, j >= 0)
         return 0
 
     lax.fori_loop(0, NX, far_turn, 0)
+    value_relay(past_a)
+    value_relay(past_b)
 
     @when(row_far < y)
     def _():
-        row_weights(row_far)
+        row_scores(row_far, False)
+
+    value_relay(row_far)
 
     for h in range(NX):
         @when(h != x)
@@ -355,24 +351,16 @@
     for dy in range(1, NY):
         state_along(dy, y).start()
 
-    value_take(NY // 2 - 1)
-    value_take(NY // 2 + 1)
-    value_take(NY // 2)
-
-    top = stat_m[0]
-    for r in range(1, NY):
-        top = jnp.maximum(top, stat_m[r])
-    total = jnp.zeros((8, WIDE), F32)
-    dots = jnp.zeros((8, WIDE), F32)
-    for r in range(NY):
-        factor = jnp.exp2((stat_m[r] - top) * (SCALE * LOG2E))
-        total = total + factor * stat_l[r]
-        dots = dots + factor * stat_t[r]
-        stat_m[r] = factor
-    inverse = 1.0 / total
-    dot_ref[...] = dots * inverse
-    for r in range(NY):
-        stat_l[r] = stat_m[r] * inverse
+    value_take(past_a)
+    value_take(past_b)
+    value_take(row_far)
+
+    top = jnp.max(stat_m[...], axis=0, keepdims=True)
+    factor = jnp.exp2((stat_m[...] - top) * (SCALE * LOG2E))
+    inverse = 1.0 / jnp.sum(factor * stat_l[...], axis=0, keepdims=True)
+    dots = jnp.sum(factor * stat_t[...], axis=0, keepdims=True) * inverse
+    dot_ref[...] = jnp.broadcast_to(dots, dot_ref.shape)
+    stat_l[...] = factor * inverse
 
     def state_back(b, owner):
         return push(lout.at[b], fin.at[owner], l3_s.at[b], l3_r.at[owner], at(y, b))
@@ -416,24 +404,31 @@
     def grad_sent(row, turn, sender, far):
         return jnp.where(turn < 0, row < sender, row < far)
 
-    def dv_across(row, dx):
+    def dv_across(row, i, straight):
+        owner = col((sigma, -sigma, 2)[i])
+        target = owner if i < 2 else jnp.where(straight, owner, col(sigma))
         return push(
-            dvp.at[row, col(dx)], vr.at[row, dx - 1], du_s.at[row, dx - 1], du_r.at[row, dx - 1],
-            at(y, col(dx)),
-        )
-
-    def dv_along(row, owner):
-        return push(vsum.at[row], vfin.at[owner], dw_s.at[row], dw_r.at[owner], at(row, x))
+            dvp.at[row, owner], vr.at[row, i], du_s.at[row, i], du_r.at[row, i], at(y, target)
+        )
+
+    def dv_ring(place, turn):
+        return push(
+            vsum.at[place], vfin.at[place], dw_s.at[place], dw_r.at[place], at(ring(y + turn), x)
+        )
+
+    def dv_relay(row):
+        @when(row <= y)
+        def _():
+            dv_across(row, 2, False).wait_recv()
+            dvp[row, col(sigma)] = (
+                dvp[row, col(sigma)].astype(F32) + vr[row, 2].astype(F32)
+            ).astype(BF16)
+            dv_across(row, 0, False).start()
 
     def dv_sum(row):
-        for dx in range(1, NX):
-            dv_across(row, dx).wait_recv()
-        return (
-            dvp[row, x].astype(F32)
-            + vr[row, 0].astype(F32)
-            + vr[row, 1].astype(F32)
-            + vr[row, 2].astype(F32)
-        )
+        dv_across(row, 0, False).wait_recv()
+        dv_across(row, 1, False).wait_recv()
+        return dvp[row, x].astype(F32) + vr[row, 0].astype(F32) + vr[row, 1].astype(F32)
 
     def place_row(place):
         forth = (lax.rem(place, 2) == 1) | (place == 0)
@@ -441,29 +436,57 @@
         far = jnp.where(forth, 4, 3)
         return turn, far, ring(y + turn * (4 - lax.div(place + 1, 2)))
 
+    def earlier(place):
+        return jnp.where(place == 1, 0, jnp.maximum(place - 2, 0))
+
+    def dv_turn(place):
+        turn, far, row = place_row(place)
+        sends = grad_sent(row, turn, y, far)
+
+        @when(row < y)
+        def _():
+            vacc[...] = dv_sum(row)
+
+        @when(row > y)
+        def _():
+            vacc[...] = jnp.zeros_like(vacc)
+
+        @when((place != 0) & (place != 2) & grad_sent(row, turn, ring(y - turn), far))
+        def _():
+            dv_ring(earlier(place), turn).wait_recv()
+            vacc[...] += vfin[earlier(place)].astype(F32)
+
+        @when(sends)
+        def _():
+            vsum[place] = vacc[...].astype(BF16)
+            dv_ring(place, turn).start()
+
     def back_turn(place, _):
         turn, far, row = place_row(place)
 
         @when(row <= y)
         def _():
-            def weigh(i, _):
-                rows = pl.ds(pl.multiple_of(i * CHUNK, CHUNK), CHUNK)
-                weights = e_ref[row, rows, :] * stat_l[row, 0:1, :]
-                wb_ref[rows, :] = weights.astype(BF16)
-                ds_ref[rows, :] = (weights * (dp_ref[row, rows, :] - dot_ref[0:1, :])).astype(BF16)
-                return 0
-
-            lax.fori_loop(0, SPAN // CHUNK, weigh, 0)
-            dkf[...] = (mm(ds_ref[...], qs[...]) * SCALE).reshape(NX, ROWS, DH)
-            dvp[row] = mm(wb_ref[...], gs[...]).astype(BF16).reshape(NX, ROWS, DH)
-            for dx in range(1, NX):
-                dv_across(row, dx).start()
+            for b in range(NX):
+                rows = slice(b * ROWS, (b + 1) * ROWS)
+                for cols in halves:
+                    weights = e_ref[row, rows, cols] * stat_l[pl.ds(row * NX + b, 1), cols]
+                    grads = weights * (dp_ref[row, rows, cols] - dot_ref[0:1, cols])
+                    wb_ref[rows, cols] = weights.astype(BF16)
+                    ds_ref[rows, cols] = grads.astype(BF16)
+                dkf[b] = mm(ds_ref[rows, :], qs[...]) * SCALE
+                dvp[row, b] = mm(wb_ref[rows, :], gs[...]).astype(BF16)
+            dv_across(row, 2, place == NY - 1).start()
+            dv_across(row, 1, False).start()
+
+            @when(place == NY - 1)
+            def _():
+                dv_across(row, 0, False).start()
 
         @when(row > y)
         def _():
             dkf[...] = jnp.zeros_like(dkf)
 
-        before = jnp.where(place == 1, 0, jnp.maximum(place - 2, 0))
+        before = earlier(place)
         takes = (place != 0) & (place != 2) & (place != NY - 1)
         takes = takes & grad_sent(row, turn, ring(y - turn), far)
         sends = (place < NY - 1) & grad_sent(row, turn, y, far)
@@ -490,12 +513,11 @@
 
         @when(place >= 1)
         def _():
-            _, _, before_row = place_row(place - 1)
-
-            @when(before_row < y)
-            def _():
-                vsum[before_row] = dv_sum(before_row).astype(BF16)
-                dv_along(before_row, y).start()
+            dv_relay(place_row(place - 1)[2])
+
+        @when(place >= 2)
+        def _():
+            dv_turn(place - 2)
 
         @when(place == 2)
         def _():
@@ -524,7 +546,9 @@
         dv_l[:, cols] = (intra[3, :, cols] + fading * mm(kh, later)).astype(BF16)
         return 0
 
-    lax.fori_loop(0, HEADS, light_out, 0)
+    lax.fori_loop(0, HEADS // 2, light_out, 0)
+    dv_turn(NY - 2)
+    lax.fori_loop(HEADS // 2, HEADS, light_out, 0)
     moves = [(o_l, o_hbm), (dq_l, dq_hbm), (dk_l, dk_hbm), (dv_l, dv_hbm)]
     moves += [(o_s, os_hbm), (dq_s, dqs_hbm), (dk_s, dks_hbm), (dv_s, dvs_hbm)]
     stores = [
@@ -532,6 +556,44 @@
     ]
     for store in stores[:4]:
         store.start()
+
+    for dx in range(1, NX):
+        key_across(dx, x).wait_send()
+
+    def sent_turn(place, _):
+        odd = lax.rem(place, 2) == 1
+        turn = jnp.where(odd, sigma, -sigma)
+        row = ring(y - turn * (lax.div(place + 1, 2) - 1))
+
+        @when(wanted(row, turn, ring(y + turn), jnp.where(odd, 4, 3)))
+        def _():
+            for j in range(NX + 1):
+                key_ring(place, row, j, turn).wait_send()
+
+        turn_back, far_back, row_back = place_row(place - 1)
+
+        @when(grad_sent(row_back, turn_back, y, far_back))
+        def _():
+            for j in range(NX):
+                grad_ring(place - 1, j, turn_back).wait_send()
+            dv_ring(place - 1, turn_back).wait_send()
+
+        return 0
+
+    lax.fori_loop(1, NY, sent_turn, 0)
+    for dy in range(1, NY):
+        state_along(dy, y).wait_send()
+    for b in range(NX):
+        @when(b != x)
+        def _():
+            light_send(b, x).wait_send()
+            state_back(b, x).wait_send()
+    for row in range(NY):
+        @when(row <= y)
+        def _():
+            for i in range(3):
+                value_across(row, i, x).wait_send()
+                dv_across(row, i, False).wait_send()
 
     def dk_across(dx):
         return push(
@@ -555,13 +617,14 @@
     stores[4].start()
     stores[5].start()
 
-    cp[...] = dv_sum(y)
-    for yy in range(1, NY):
-        @when(yy > y)
-        def _():
-            push(vsum.at[yy], vfin.at[yy], dw_s.at[yy], dw_r.at[yy], at(yy, x)).wait_recv()
-            cp[...] += vfin[yy].astype(F32)
-    dv_s[...] = cp[...].astype(BF16)
+    dv_across(y, 2, True).wait_recv()
+    vacc[...] = dv_sum(y) + vr[y, 2].astype(F32)
+    for place, turn, far in ((NY - 3, sigma, 4), (NY - 2, -sigma, 3)):
+        @when(grad_sent(y, turn, ring(y - turn), far))
+        def _():
+            dv_ring(place, turn).wait_recv()
+            vacc[...] += vfin[place].astype(F32)
+    dv_s[...] = vacc[...].astype(BF16)
     stores[7].start()
 
     for dx in range(1, NX):
@@ -572,61 +635,24 @@
     stores[6].start()
 
     for dx in range(1, NX):
-        key_across(dx, x).wait_send()
         dk_across(dx).wait_send()
-
-    def sent_turn(place, _):
-        odd = lax.rem(place, 2) == 1
-        turn = jnp.where(odd, sigma, -sigma)
-        row = ring(y - turn * (lax.div(place + 1, 2) - 1))
-
-        @when(wanted(row, turn, ring(y + turn), jnp.where(odd, 4, 3)))
-        def _():
-            for j in range(NX):
-                key_ring(place, row, j, turn).wait_send()
-
-        turn_back, far_back, row_back = place_row(place - 1)
-
-        @when(grad_sent(row_back, turn_back, y, far_back))
-        def _():
-            for j in range(NX):
-                grad_ring(place - 1, j, turn_back).wait_send()
-
-        return 0
-
-    lax.fori_loop(1, NY, sent_turn, 0)
-    for dy in range(1, NY):
-        state_along(dy, y).wait_send()
-
-        @when(y + dy < NY)
-        def _():
-            value_along(dy, y).wait_send()
-
-        @when(dy - 1 < y)
-        def _():
-            dv_along(dy - 1, y).wait_send()
-    for b in range(NX):
-        @when(b != x)
-        def _():
-            light_send(b, x).wait_send()
-            state_back(b, x).wait_send()
-    for dy in range(NY):
-        @when(dy <= y)
-        def _():
-            for dx in range(1, NX):
-                value_across(dy, dx, ring(y - dy), x).wait_send()
-                dv_across(dy, dx).wait_send()
     for store in stores:
         store.wait()
 
 
 def copy_out(*refs):
-    ins, outs, sems = refs[:8], refs[8:16], refs[16]
-    copies = [pltpu.make_async_copy(a, b, sems.at[n]) for n, (a, b) in enumerate(zip(ins, outs))]
-    for copy in copies:
-        copy.start()
-    for copy in copies:
-        copy.wait()
+    ins, outs, held, sems = refs[:8], refs[8:16], refs[16:24], refs[24]
+    reads = [pltpu.make_async_copy(a, b, sems.at[0, n]) for n, (a, b) in enumerate(zip(ins, held))]
+    writes = [
+        pltpu.make_async_copy(a, b, sems.at[1, n]) for n, (a, b) in enumerate(zip(held, outs))
+    ]
+    for read in reads:
+        read.start()
+    for read, write in zip(reads, writes):
+        read.wait()
+        write.start()
+    for write in writes:
+        write.wait()
 
 
 def shards(q_light, k_light, v_light, g_light, log_decay, q_soft, k_soft, v_soft, g_soft):
@@ -648,9 +674,9 @@
         pltpu.VMEM((NY, NX, ROWS, DH), BF16),
         pltpu.VMEM((NY, SPAN, WIDE), F32),
         pltpu.VMEM((NY, SPAN, WIDE), F32),
-        pltpu.VMEM((NY, 8, WIDE), F32),
-        pltpu.VMEM((NY, 8, WIDE), F32),
-        pltpu.VMEM((NY, 8, WIDE), F32),
+        pltpu.VMEM((NY * NX, WIDE), F32),
+        pltpu.VMEM((NY * NX, WIDE), F32),
+        pltpu.VMEM((NY * NX, WIDE), F32),
         pltpu.VMEM((8, WIDE), F32),
         pltpu.VMEM((SPAN, WIDE), BF16),
         pltpu.VMEM((SPAN, WIDE), BF16),
@@ -661,8 +687,9 @@
         pltpu.VMEM((NY - 1, NX, ROWS, DH), BF16),
         pltpu.VMEM((NY, NX, ROWS, DH), BF16),
         pltpu.VMEM((NY, NX - 1, ROWS, DH), BF16),
-        pltpu.VMEM((NY, ROWS, DH), BF16),
-        pltpu.VMEM((NY, ROWS, DH), BF16),
+        pltpu.VMEM((NY - 1, ROWS, DH), BF16),
+        pltpu.VMEM((NY - 1, ROWS, DH), BF16),
+        pltpu.VMEM((ROWS, DH), F32),
         pltpu.VMEM((NX - 1, ROWS, DH), BF16),
         pltpu.VMEM((NX, ROWS, DH), BF16),
         pltpu.VMEM((HEADS, ROWS), F32),
@@ -679,15 +706,14 @@
         dma((15,)),
         dma((8,)),
         dma((NX - 1,)), dma((NX - 1,)),
-        dma((NY - 1, NX)), dma((NY - 1, NX)),
-        dma((NY - 1,)), dma((NY - 1,)),
+        dma((NY - 1, NX + 1)), dma((NY - 1, NX + 1)),
         dma((NY, NX - 1)), dma((NY, NX - 1)),
         dma((NX,)), dma((NX,)),
         dma((NY - 1,)), dma((NY - 1,)),
         dma((NX,)), dma((NX,)),
         dma((NY - 1, NX)), dma((NY - 1, NX)),
         dma((NY, NX - 1)), dma((NY, NX - 1)),
-        dma((NY,)), dma((NY,)),
+        dma((NY - 1,)), dma((NY - 1,)),
         dma((NX - 1,)), dma((NX - 1,)),
     ]
     hbm = pl.BlockSpec(memory_space=pltpu.HBM)
@@ -708,7 +734,7 @@
         out_shape=shapes,
         in_specs=[hbm] * 8,
         out_specs=(hbm,) * 8,
-        scratch_shapes=[dma((8,))],
+        scratch_shapes=[pltpu.VMEM(shape.shape, BF16) for shape in shapes] + [dma((2, 8))],
         compiler_params=pltpu.CompilerParams(vmem_limit_bytes=room),
     )(*results)
 

time: 92.9 us -> 71.5 us (0.77)
  the two profiles are of different devices: /device:TPU:256 before, /device:TPU:312 now
where the time goes in v3:
time: 71.5 us; the launch traced here: 71.3 us
  Pallas kernels  70.7 us (99%)
    pallas_call x1, Pallas kernels, shards(): pl.pallas_call(kernel, out_shape=shapes, in_specs=[hbm] * 9, out_specs=(h...  68.7 us
    pallas_call x1, Pallas kernels, shards(): pl.pallas_call(copy_out, out_shape=shapes, in_specs=[hbm] * 8, out_specs=...  2.02 us

profile of v3, /device:TPU:312, one launch (start us, length us, event | category | flops | bytes accessed | tf_op | source)
XLA Modules:
  0.0 71.3 jit_solution(16586194042601134328)
XLA Ops:
  0.6 68.7 %shard_map.152 = (bf16[128,512]{1,0:T(8,128)(2,1)}, bf16[128,512]{1,0:T(8,128)(2,1)}, bf16[128,512]{1,0:T(8,128)(2,1)}, bf16[128,512]{1,0:T(8,128)(2,1)}, bf16[1...) custom-call(bf16[128,512]{1,0:T(8,128)(2,1)} %q_hbm.1, ...), custom_call_target="tpu_custom_call" | custom-call | tf_op jit(solution)/shard_map/pallas_call | solution.py:722
  69.3 2.0 %shard_map.153 = (bf16[128,512]{1,0:T(8,128)(2,1)}, bf16[128,512]{1,0:T(8,128)(2,1)}, bf16[128,512]{1,0:T(8,128)(2,1)}, bf16[128,512]{1,0:T(8,128)(2,1)}, bf16[1...) custom-call(bf16[128,512]{1,0:T(8,128)(2,1)} %get-tuple-element.16.refs_0_, ...), custom_call_target="tpu_custom_call" | custom-call | tf_op jit(solution)/shard_map/pallas_call | solution.py:732

commit v4 on v3

--- a/solution.py
+++ b/solution.py
@@ -73,7 +73,7 @@
     me = lax.axis_index("ctx")
     y = lax.div(me, NX)
     x = lax.rem(me, NX)
-    sigma = 1 - 2 * lax.rem(lax.axis_index("tp"), 2)
+    sigma = -1
 
     def ring(value):
         return lax.rem(value + 2 * NY, NY)

time: 71.5 us -> 73.1 us (1.022)
  the two profiles are of different devices: /device:TPU:312 before, /device:TPU:320 now
where the time goes in v4:
time: 73.1 us; the launch traced here: 72.9 us
  Pallas kernels  72.3 us (99%)
    pallas_call x1, Pallas kernels, shards(): pl.pallas_call(kernel, out_shape=shapes, in_specs=[hbm] * 9, out_specs=(h...  70.3 us
    pallas_call x1, Pallas kernels, shards(): pl.pallas_call(copy_out, out_shape=shapes, in_specs=[hbm] * 8, out_specs=...  2.02 us

profile of v4, /device:TPU:320, one launch (start us, length us, event | category | flops | bytes accessed | tf_op | source)
XLA Modules:
  0.0 72.9 jit_solution(2240748027855020500)
XLA Ops:
  0.6 70.3 %shard_map.152 = (bf16[128,512]{1,0:T(8,128)(2,1)}, bf16[128,512]{1,0:T(8,128)(2,1)}, bf16[128,512]{1,0:T(8,128)(2,1)}, bf16[128,512]{1,0:T(8,128)(2,1)}, bf16[1...) custom-call(bf16[128,512]{1,0:T(8,128)(2,1)} %q_hbm.1, ...), custom_call_target="tpu_custom_call" | custom-call | tf_op jit(solution)/shard_map/pallas_call | solution.py:722
  70.9 2.0 %shard_map.153 = (bf16[128,512]{1,0:T(8,128)(2,1)}, bf16[128,512]{1,0:T(8,128)(2,1)}, bf16[128,512]{1,0:T(8,128)(2,1)}, bf16[128,512]{1,0:T(8,128)(2,1)}, bf16[1...) custom-call(bf16[128,512]{1,0:T(8,128)(2,1)} %get-tuple-element.16.refs_0_, ...), custom_call_target="tpu_custom_call" | custom-call | tf_op jit(solution)/shard_map/pallas_call | solution.py:732

commit v5 on v3

--- a/solution.py
+++ b/solution.py
@@ -62,10 +62,11 @@
     q_hbm, k_hbm, v_hbm, g_hbm, ld_hbm, qs_hbm, ks_hbm, vs_hbm, gs_hbm,
     o_hbm, dq_hbm, dk_hbm, dv_hbm, os_hbm, dqs_hbm, dks_hbm, dvs_hbm,
     o_l, dq_l, dk_l, dv_l, o_s, dq_s, dk_s, dv_s,
-    q_l, k_l, v_l, g_l, ld, qs, gs, qs_t, gs_t,
+    q_l, k_l, v_l, g_l, ld, qa, ga, ohead, oin, qs, gs, qs_t, gs_t,
     kg, vg, e_ref, dp_ref, stat_m, stat_l, stat_t, dot_ref, wb_ref, ds_ref,
     out_t, dq_t, dkf, dkp, rbuf, dvp, vr, vsum, vfin, vacc, kfin, dks,
     lrow, lall, intra, lmsg, lin, ymsg, yin, cp, cg, lout, fin,
+    qx_s, qx_r, ox_s, ox_r,
     in_s, out_s, kx_s, kx_r, kr_s, kr_r, vx_s, vx_r,
     l1_s, l1_r, y_s, y_r, l3_s, l3_r,
     dr_s, dr_r, du_s, du_r, dw_s, dw_r, kf_s, kf_r,
@@ -75,6 +76,10 @@
     x = lax.rem(me, NX)
     sigma = 1 - 2 * lax.rem(lax.axis_index("tp"), 2)
 
+    side = jnp.where(y < NY // 2, 0, 1)
+    low = jnp.minimum(y, NY - 1 - y)
+    high = NY - 1 - low
+
     def ring(value):
         return lax.rem(value + 2 * NY, NY)
 
@@ -101,8 +106,8 @@
 
     parts = [slice(h * DH, (h + 1) * DH) for h in range(HEADS)]
     moves = [(ks_hbm, kg.at[y, x]), (vs_hbm, vg.at[y, x]), (ld_hbm, ld)]
-    moves += [(qs_hbm.at[:, part], qs.at[part, :]) for part in parts]
-    moves += [(gs_hbm.at[:, part], gs.at[part, :]) for part in parts]
+    moves += [(qs_hbm.at[:, part], qa.at[h]) for h, part in enumerate(parts)]
+    moves += [(gs_hbm.at[:, part], ga.at[h]) for h, part in enumerate(parts)]
     moves += [(q_hbm, q_l), (k_hbm, k_l), (v_hbm, v_l), (g_hbm, g_l)]
     fetches = [
         pltpu.make_async_copy(src, dst, in_s.at[n]) for n, (src, dst) in enumerate(moves)
@@ -118,8 +123,10 @@
     dq_t[...] = jnp.zeros_like(dq_t)
     cp[...] = jnp.zeros_like(cp)
     cg[...] = jnp.zeros_like(cg)
-    for fetch in fetches[:3]:
+    for fetch in fetches[:11]:
         fetch.wait()
+    qs[side] = qa[pl.ds(2 * side, 2)]
+    gs[side] = ga[pl.ds(2 * side, 2)]
     pl.semaphore_wait(barrier, NX + NY - 2)
 
     def key_across(dx, owner):
@@ -127,10 +134,17 @@
             kg.at[y, owner], kg.at[y, owner], kx_s.at[dx - 1], kx_r.at[dx - 1], at(y, col(dx))
         )
 
-    def value_across(row, i, owner):
-        return push(
-            vg.at[row, owner], vg.at[row, owner], vx_s.at[row, i], vx_r.at[row, i],
-            at(y, col(-sigma if i == 1 else sigma)),
+    def value_across(row, dx, owner):
+        return push(
+            vg.at[row, owner], vg.at[row, owner], vx_s.at[row, dx - 1], vx_r.at[row, dx - 1],
+            at(y, col(dx)),
+        )
+
+    def query_swap(n):
+        src, dst = ((qa, qs), (ga, gs))[n]
+        return push(
+            src.at[pl.ds(2 - 2 * side, 2)], dst.at[side], qx_s.at[n], qx_r.at[n],
+            at(NY - 1 - y, x),
         )
 
     def key_ring(place, row, j, turn):
@@ -140,36 +154,55 @@
             block, block, kr_s.at[place - 1, j], kr_r.at[place - 1, j], at(ring(y + turn), x)
         )
 
-    def wanted(row, turn, target, far):
-        return jnp.where(turn > 0, row < target, row < far)
-
-    def key_start(place, row, j, turn, far):
-        @when(wanted(row, turn, ring(y + turn), far))
-        def _():
-            key_ring(place, row, j, turn).start()
-
     for dx in range(1, NX):
         key_across(dx, x).start()
     for j in (NX, 0):
-        key_start(1, y, j, sigma, 4)
-        key_start(2, y, j, -sigma, 3)
-    value_across(y, 0, x).start()
-    value_across(y, 1, x).start()
-
-    def row_scores(row, masked):
+        key_ring(1, y, j, sigma).start()
+        key_ring(2, y, j, -sigma).start()
+    for n in range(2):
+        query_swap(n).start()
+    for dx in range(1, NX):
+        value_across(y, dx, x).start()
+
+    def part_scores(row, s, masked):
+        for b in range(NX):
+            scores = mm(kg[row, b], qs_t[s])
+            if masked:
+                key_at = lax.broadcasted_iota(jnp.int32, scores.shape, 0) + b * ROWS
+                query_at = lax.rem(lax.broadcasted_iota(jnp.int32, scores.shape, 1), ROWS)
+                scores = jnp.where(key_at <= query_at + x * ROWS, scores, MASKED)
+            top = jnp.max(scores, axis=0, keepdims=True)
+            grown = jnp.exp2(scores * (SCALE * LOG2E) - top * (SCALE * LOG2E))
+            e_ref[row, b * ROWS : (b + 1) * ROWS, halves[s]] = grown
+            stat_m[pl.ds(row * NX + b, 1), halves[s]] = top
+            stat_l[pl.ds(row * NX + b, 1), halves[s]] = jnp.sum(grown, axis=0, keepdims=True)
+
+    def row_scores(row):
+        @when(row < low)
+        def _():
+            part_scores(row, 0, False)
+            part_scores(row, 1, False)
+
+        @when(row == low)
+        def _():
+            part_scores(row, 0, True)
+            part_scores(row, 1, False)
+
+        @when((row > low) & (row < high))
+        def _():
+            part_scores(row, 1, False)
+
+        @when(row == high)
+        def _():
+            part_scores(row, 1, True)
+
+    def part_grads(row, s):
         for b in range(NX):
             rows = slice(b * ROWS, (b + 1) * ROWS)
-            for cols in halves:
-                scores = mm(kg[row, b], qs_t[:, cols])
-                if masked:
-                    key_at = lax.broadcasted_iota(jnp.int32, scores.shape, 0) + b * ROWS
-                    query_at = lax.rem(lax.broadcasted_iota(jnp.int32, scores.shape, 1), ROWS)
-                    scores = jnp.where(key_at <= query_at + x * ROWS, scores, MASKED)
-                top = jnp.max(scores, axis=0, keepdims=True)
-                grown = jnp.exp2(scores * (SCALE * LOG2E) - top * (SCALE * LOG2E))
-                e_ref[row, rows, cols] = grown
-                stat_m[pl.ds(row * NX + b, 1), cols] = top
-                stat_l[pl.ds(row * NX + b, 1), cols] = jnp.sum(grown, axis=0, keepdims=True)
+            grads = mm(vg[row, b], gs_t[s])
+            dp_ref[row, rows, halves[s]] = grads
+            weighed = jnp.sum(grads * e_ref[row, rows, halves[s]], axis=0, keepdims=True)
+            stat_t[pl.ds(row * NX + b, 1), halves[s]] = weighed
 
     def light_send(h, owner):
         return push(lmsg.at[h], lin.at[owner], l1_s.at[h], l1_r.at[owner], at(y, h))
@@ -213,53 +246,54 @@
     lrow[...] = jnp.dot(
         ld[...], upper, precision=lax.Precision.HIGHEST, preferred_element_type=F32
     )
-    for fetch in fetches[3:]:
+    for fetch in fetches[11:]:
         fetch.wait()
-    for part in parts:
-        qs_t[:, part] = qs[part, :].T
-        gs_t[:, part] = gs[part, :].T
+
+    def turned(s):
+        for i in range(2):
+            qs_t[s, :, i * ROWS : (i + 1) * ROWS] = qs[s, i].T
+            gs_t[s, :, i * ROWS : (i + 1) * ROWS] = gs[s, i].T
+
+    turned(side)
 
     for j in range(1, NX):
         key_across(j, col(-j)).wait_recv()
-        key_start(1, y, j, sigma, 4)
-        key_start(2, y, j, -sigma, 3)
-    row_scores(y, True)
+        key_ring(1, y, j, sigma).start()
+        key_ring(2, y, j, -sigma).start()
     light_head(0)
+    for n in range(2):
+        query_swap(n).wait_recv()
+    turned(1 - side)
+    row_scores(y)
     light_head(1)
 
-    def key_take(place, row, j, turn, far, last):
-        @when(wanted(row, turn, y, far))
-        def _():
-            key_ring(place, row, j, turn).wait_recv()
-
-            @when(jnp.logical_not(last))
-            def _():
-                key_start(place + 2, row, j, turn, far)
+    def key_take(place, row, j, turn, last):
+        key_ring(place, row, j, turn).wait_recv()
+
+        @when(jnp.logical_not(last))
+        def _():
+            key_ring(place + 2, row, j, turn).start()
 
     def value_pass(row):
-        @when(row < y)
-        def _():
-            value_across(row, 0, x).start()
-            value_across(row, 1, x).start()
-
-    def value_relay(row):
-        @when(row <= y)
-        def _():
-            value_across(row, 0, col(-sigma)).wait_recv()
-            value_across(row, 2, col(-sigma)).start()
+        @when(row <= high)
+        def _():
+            for dx in range(1, NX):
+                value_across(row, dx, x).start()
 
     def value_take(row):
-        @when(row <= y)
-        def _():
-            value_across(row, 1, col(sigma)).wait_recv()
-            value_across(row, 2, col(2)).wait_recv()
-            for b in range(NX):
-                rows = slice(b * ROWS, (b + 1) * ROWS)
-                for cols in halves:
-                    grads = mm(vg[row, b], gs_t[:, cols])
-                    dp_ref[row, rows, cols] = grads
-                    weighed = jnp.sum(grads * e_ref[row, rows, cols], axis=0, keepdims=True)
-                    stat_t[pl.ds(row * NX + b, 1), cols] = weighed
+        @when(row <= high)
+        def _():
+            for dx in range(1, NX):
+                value_across(row, dx, col(-dx)).wait_recv()
+
+        @when(row <= low)
+        def _():
+            part_grads(row, 0)
+            part_grads(row, 1)
+
+        @when((row > low) & (row <= high))
+        def _():
+            part_grads(row, 1)
 
     def rows_at(k):
         return ring(y - sigma * k), ring(y + sigma * k)
@@ -267,30 +301,19 @@
     def gather_turn(k, _):
         row_a, row_b = rows_at(k)
         past_a, past_b = rows_at(k - 1)
-        key_take(2 * k - 1, row_a, NX, sigma, 4, k < 0)
+        key_take(2 * k - 1, row_a, NX, sigma, k < 0)
         value_pass(row_a)
-        key_take(2 * k, row_b, NX, -sigma, 3, k == 3)
+        key_take(2 * k, row_b, NX, -sigma, k == 3)
         value_pass(row_b)
 
         def block_turn(j, _):
-            key_take(2 * k - 1, row_a, j, sigma, 4, k < 0)
-            key_take(2 * k, row_b, j, -sigma, 3, k == 3)
+            key_take(2 * k - 1, row_a, j, sigma, k < 0)
+            key_take(2 * k, row_b, j, -sigma, k == 3)
             return 0
 
         lax.fori_loop(0, NX, block_turn, 0)
-        value_relay(past_a)
-
-        @when(k > 1)
-        def _():
-            value_relay(past_b)
-
-        @when(row_a < y)
-        def _():
-            row_scores(row_a, False)
-
-        @when(row_b < y)
-        def _():
-            row_scores(row_b, False)
+        row_scores(row_a)
+        row_scores(row_b)
 
         @when(k < 3)
         def _():
@@ -307,22 +330,15 @@
     lax.fori_loop(1, NY // 2, gather_turn, 0)
     past_a, past_b = rows_at(NY // 2 - 1)
     row_far = ring(y - sigma * (NY // 2))
-    key_take(NY - 1, row_far, NX, sigma, 4, row_far >= 0)
+    key_take(NY - 1, row_far, NX, sigma, row_far >= 0)
     value_pass(row_far)
 
     def far_turn(j, _):
-        key_take(NY - 1, row_far, j, sigma, 4, j >= 0)
+        key_take(NY - 1, row_far, j, sigma, j >= 0)
         return 0
 
     lax.fori_loop(0, NX, far_turn, 0)
-    value_relay(past_a)
-    value_relay(past_b)
-
-    @when(row_far < y)
-    def _():
-        row_scores(row_far, False)
-
-    value_relay(row_far)
+    row_scores(row_far)
 
     for h in range(NX):
         @when(h != x)
@@ -401,14 +417,10 @@
             at(ring(y + turn), x),
         )
 
-    def grad_sent(row, turn, sender, far):
-        return jnp.where(turn < 0, row < sender, row < far)
-
-    def dv_across(row, i, straight):
-        owner = col((sigma, -sigma, 2)[i])
-        target = owner if i < 2 else jnp.where(straight, owner, col(sigma))
-        return push(
-            dvp.at[row, owner], vr.at[row, i], du_s.at[row, i], du_r.at[row, i], at(y, target)
+    def dv_across(row, dx):
+        return push(
+            dvp.at[row, col(dx)], vr.at[row, dx - 1], du_s.at[row, dx - 1], du_r.at[row, dx - 1],
+            at(y, col(dx)),
         )
 
     def dv_ring(place, turn):
@@ -416,80 +428,84 @@
             vsum.at[place], vfin.at[place], dw_s.at[place], dw_r.at[place], at(ring(y + turn), x)
         )
 
-    def dv_relay(row):
-        @when(row <= y)
-        def _():
-            dv_across(row, 2, False).wait_recv()
-            dvp[row, col(sigma)] = (
-                dvp[row, col(sigma)].astype(F32) + vr[row, 2].astype(F32)
-            ).astype(BF16)
-            dv_across(row, 0, False).start()
-
     def dv_sum(row):
-        dv_across(row, 0, False).wait_recv()
-        dv_across(row, 1, False).wait_recv()
-        return dvp[row, x].astype(F32) + vr[row, 0].astype(F32) + vr[row, 1].astype(F32)
+        for dx in range(1, NX):
+            dv_across(row, dx).wait_recv()
+        return (
+            dvp[row, x].astype(F32)
+            + vr[row, 0].astype(F32)
+            + vr[row, 1].astype(F32)
+            + vr[row, 2].astype(F32)
+        )
 
     def place_row(place):
         forth = (lax.rem(place, 2) == 1) | (place == 0)
         turn = jnp.where(forth, sigma, -sigma)
-        far = jnp.where(forth, 4, 3)
-        return turn, far, ring(y + turn * (4 - lax.div(place + 1, 2)))
+        return turn, ring(y + turn * (4 - lax.div(place + 1, 2)))
 
     def earlier(place):
         return jnp.where(place == 1, 0, jnp.maximum(place - 2, 0))
 
     def dv_turn(place):
-        turn, far, row = place_row(place)
-        sends = grad_sent(row, turn, y, far)
-
-        @when(row < y)
+        turn, row = place_row(place)
+
+        @when(row <= high)
         def _():
             vacc[...] = dv_sum(row)
 
-        @when(row > y)
+        @when(row > high)
         def _():
             vacc[...] = jnp.zeros_like(vacc)
 
-        @when((place != 0) & (place != 2) & grad_sent(row, turn, ring(y - turn), far))
+        @when((place != 0) & (place != 2))
         def _():
             dv_ring(earlier(place), turn).wait_recv()
             vacc[...] += vfin[earlier(place)].astype(F32)
 
-        @when(sends)
-        def _():
-            vsum[place] = vacc[...].astype(BF16)
-            dv_ring(place, turn).start()
+        vsum[place] = vacc[...].astype(BF16)
+        dv_ring(place, turn).start()
+
+    def back_part(row, sides):
+        for b in range(NX):
+            rows = slice(b * ROWS, (b + 1) * ROWS)
+            dk_part, dv_part = 0.0, 0.0
+            for s in sides:
+                cols = halves[s]
+                weights = e_ref[row, rows, cols] * stat_l[pl.ds(row * NX + b, 1), cols]
+                grads = weights * (dp_ref[row, rows, cols] - dot_ref[0:1, cols])
+                wb_ref[rows, cols] = weights.astype(BF16)
+                ds_ref[rows, cols] = grads.astype(BF16)
+                dk_part += mm(ds_ref[rows, cols], qs[s].reshape(2 * ROWS, DH))
+                dv_part += mm(wb_ref[rows, cols], gs[s].reshape(2 * ROWS, DH))
+            dkf[b] = dk_part * SCALE
+            dvp[row, b] = dv_part.astype(BF16)
+        for dx in range(1, NX):
+            dv_across(row, dx).start()
+
+    def query_part(row, sides):
+        values_t = vg[row].reshape(SPAN, DH)
+        keys_t = kg[row].reshape(SPAN, DH)
+        for s in sides:
+            out_t[s] += mm_tn(values_t, wb_ref[:, halves[s]])
+            dq_t[s] += mm_tn(keys_t, ds_ref[:, halves[s]])
 
     def back_turn(place, _):
-        turn, far, row = place_row(place)
-
-        @when(row <= y)
-        def _():
-            for b in range(NX):
-                rows = slice(b * ROWS, (b + 1) * ROWS)
-                for cols in halves:
-                    weights = e_ref[row, rows, cols] * stat_l[pl.ds(row * NX + b, 1), cols]
-                    grads = weights * (dp_ref[row, rows, cols] - dot_ref[0:1, cols])
-                    wb_ref[rows, cols] = weights.astype(BF16)
-                    ds_ref[rows, cols] = grads.astype(BF16)
-                dkf[b] = mm(ds_ref[rows, :], qs[...]) * SCALE
-                dvp[row, b] = mm(wb_ref[rows, :], gs[...]).astype(BF16)
-            dv_across(row, 2, place == NY - 1).start()
-            dv_across(row, 1, False).start()
-
-            @when(place == NY - 1)
-            def _():
-                dv_across(row, 0, False).start()
-
-        @when(row > y)
+        turn, row = place_row(place)
+
+        @when(row <= low)
+        def _():
+            back_part(row, (0, 1))
+
+        @when((row > low) & (row <= high))
+        def _():
+            back_part(row, (1,))
+
+        @when(row > high)
         def _():
             dkf[...] = jnp.zeros_like(dkf)
 
         before = earlier(place)
         takes = (place != 0) & (place != 2) & (place != NY - 1)
-        takes = takes & grad_sent(row, turn, ring(y - turn), far)
-        sends = (place < NY - 1) & grad_sent(row, turn, y, far)
 
         def ring_block(b, _):
             @when(takes)
@@ -497,7 +513,7 @@
                 grad_ring(before, b, turn).wait_recv()
                 dkf[b] += rbuf[before, b].astype(F32)
 
-            @when(sends)
+            @when(place < NY - 1)
             def _():
                 dkp[place, b] = dkf[b].astype(BF16)
                 grad_ring(place, b, turn).start()
@@ -506,18 +522,17 @@
 
         lax.fori_loop(0, NX, ring_block, 0)
 
-        @when(row <= y)
-        def _():
-            out_t[...] += mm_tn(vg[row].reshape(SPAN, DH), wb_ref[...])
-            dq_t[...] += mm_tn(kg[row].reshape(SPAN, DH), ds_ref[...])
+        @when(row <= low)
+        def _():
+            query_part(row, (0, 1))
+
+        @when((row > low) & (row <= high))
+        def _():
+            query_part(row, (1,))
 
         @when(place >= 1)
         def _():
-            dv_relay(place_row(place - 1)[2])
-
-        @when(place >= 2)
-        def _():
-            dv_turn(place - 2)
+            dv_turn(place - 1)
 
         @when(place == 2)
         def _():
@@ -526,6 +541,18 @@
         return 0
 
     lax.fori_loop(0, NY, back_turn, 0)
+
+    def turned_back(s, i):
+        cols = slice(i * ROWS, (i + 1) * ROWS)
+        return out_t[s, :, cols].T.astype(BF16), (dq_t[s, :, cols].T * SCALE).astype(BF16)
+
+    def head_back(n):
+        return push(ohead.at[n], oin.at[n], ox_s.at[n], ox_r.at[n], at(NY - 1 - y, x))
+
+    for i in range(2):
+        ohead[0, i], ohead[1, i] = turned_back(1 - side, i)
+    for n in range(2):
+        head_back(n).start()
 
     for b in range(NX):
         @when(b != x)
@@ -546,9 +573,7 @@
         dv_l[:, cols] = (intra[3, :, cols] + fading * mm(kh, later)).astype(BF16)
         return 0
 
-    lax.fori_loop(0, HEADS // 2, light_out, 0)
-    dv_turn(NY - 2)
-    lax.fori_loop(HEADS // 2, HEADS, light_out, 0)
+    lax.fori_loop(0, HEADS, light_out, 0)
     moves = [(o_l, o_hbm), (dq_l, dq_hbm), (dk_l, dk_hbm), (dv_l, dv_hbm)]
     moves += [(o_s, os_hbm), (dq_s, dqs_hbm), (dk_s, dks_hbm), (dv_s, dvs_hbm)]
     stores = [
@@ -560,24 +585,17 @@
     for dx in range(1, NX):
         key_across(dx, x).wait_send()
 
-    def sent_turn(place, _):
+    def sent_turn(place, _carry):
         odd = lax.rem(place, 2) == 1
         turn = jnp.where(odd, sigma, -sigma)
         row = ring(y - turn * (lax.div(place + 1, 2) - 1))
 
-        @when(wanted(row, turn, ring(y + turn), jnp.where(odd, 4, 3)))
-        def _():
-            for j in range(NX + 1):
-                key_ring(place, row, j, turn).wait_send()
-
-        turn_back, far_back, row_back = place_row(place - 1)
-
-        @when(grad_sent(row_back, turn_back, y, far_back))
-        def _():
-            for j in range(NX):
-                grad_ring(place - 1, j, turn_back).wait_send()
-            dv_ring(place - 1, turn_back).wait_send()
-
+        for j in range(NX + 1):
+            key_ring(place, row, j, turn).wait_send()
+        turn_back, _ = place_row(place - 1)
+        for j in range(NX):
+            grad_ring(place - 1, j, turn_back).wait_send()
+        dv_ring(place - 1, turn_back).wait_send()
         return 0
 
     lax.fori_loop(1, NY, sent_turn, 0)
@@ -588,12 +606,15 @@
         def _():
             light_send(b, x).wait_send()
             state_back(b, x).wait_send()
+    for n in range(2):
+        query_swap(n).wait_send()
+        head_back(n).wait_send()
     for row in range(NY):
-        @when(row <= y)
-        def _():
-            for i in range(3):
-                value_across(row, i, x).wait_send()
-                dv_across(row, i, False).wait_send()
+        @when(row <= high)
+        def _():
+            for dx in range(1, NX):
+                value_across(row, dx, x).wait_send()
+                dv_across(row, dx).wait_send()
 
     def dk_across(dx):
         return push(
@@ -602,28 +623,30 @@
 
     for j in (1, 2, 3, 0):
         b = col(j)
-        for place, turn, far in ((NY - 3, sigma, 4), (NY - 2, -sigma, 3)):
-            @when(grad_sent(y, turn, ring(y - turn), far))
-            def _():
-                grad_ring(place, b, turn).wait_recv()
-                dkf[b] += rbuf[place, b].astype(F32)
+        for place, turn in ((NY - 3, sigma), (NY - 2, -sigma)):
+            grad_ring(place, b, turn).wait_recv()
+            dkf[b] += rbuf[place, b].astype(F32)
         if j:
             dks[b] = dkf[b].astype(BF16)
             dk_across(j).start()
 
-    for part in parts:
-        o_s[:, part] = out_t[:, part].T.astype(BF16)
-        dq_s[:, part] = (dq_t[:, part].T * SCALE).astype(BF16)
+    def head_cols(s, i):
+        return pl.ds(pl.multiple_of((2 * s + i) * DH, DH), DH)
+
+    for i in range(2):
+        o_s[:, head_cols(side, i)], dq_s[:, head_cols(side, i)] = turned_back(side, i)
+    for n in range(2):
+        head_back(n).wait_recv()
+    for i in range(2):
+        o_s[:, head_cols(1 - side, i)] = oin[0, i]
+        dq_s[:, head_cols(1 - side, i)] = oin[1, i]
     stores[4].start()
     stores[5].start()
 
-    dv_across(y, 2, True).wait_recv()
-    vacc[...] = dv_sum(y) + vr[y, 2].astype(F32)
-    for place, turn, far in ((NY - 3, sigma, 4), (NY - 2, -sigma, 3)):
-        @when(grad_sent(y, turn, ring(y - turn), far))
-        def _():
-            dv_ring(place, turn).wait_recv()
-            vacc[...] += vfin[place].astype(F32)
+    vacc[...] = dv_sum(y)
+    for place, turn in ((NY - 3, sigma), (NY - 2, -sigma)):
+        dv_ring(place, turn).wait_recv()
+        vacc[...] += vfin[place].astype(F32)
     dv_s[...] = vacc[...].astype(BF16)
     stores[7].start()
 
@@ -666,10 +689,14 @@
         pltpu.VMEM((ROWS, WIDE), BF16),
         pltpu.VMEM((ROWS, WIDE), BF16),
         pltpu.VMEM((HEADS, ROWS), F32),
-        pltpu.VMEM((WIDE, DH), BF16),
-        pltpu.VMEM((WIDE, DH), BF16),
-        pltpu.VMEM((DH, WIDE), BF16),
-        pltpu.VMEM((DH, WIDE), BF16),
+        pltpu.VMEM((HEADS, ROWS, DH), BF16),
+        pltpu.VMEM((HEADS, ROWS, DH), BF16),
+        pltpu.VMEM((2, 2, ROWS, DH), BF16),
+        pltpu.VMEM((2, 2, ROWS, DH), BF16),
+        pltpu.VMEM((2, 2, ROWS, DH), BF16),
+        pltpu.VMEM((2, 2, ROWS, DH), BF16),
+        pltpu.VMEM((2, DH, 2 * ROWS), BF16),
+        pltpu.VMEM((2, DH, 2 * ROWS), BF16),
         pltpu.VMEM((NY, NX, ROWS, DH), BF16),
         pltpu.VMEM((NY, NX, ROWS, DH), BF16),
         pltpu.VMEM((NY, SPAN, WIDE), F32),
@@ -680,8 +707,8 @@
         pltpu.VMEM((8, WIDE), F32),
         pltpu.VMEM((SPAN, WIDE), BF16),
         pltpu.VMEM((SPAN, WIDE), BF16),
-        pltpu.VMEM((DH, WIDE), F32),
-        pltpu.VMEM((DH, WIDE), F32),
+        pltpu.VMEM((2, DH, 2 * ROWS), F32),
+        pltpu.VMEM((2, DH, 2 * ROWS), F32),
         pltpu.VMEM((NX, ROWS, DH), F32),
         pltpu.VMEM((NY - 1, NX, ROWS, DH), BF16),
         pltpu.VMEM((NY - 1, NX, ROWS, DH), BF16),
@@ -703,6 +730,8 @@
         pltpu.VMEM((DH, DH), F32),
         pltpu.VMEM((NX, 2 * DH, DH), BF16),
         pltpu.VMEM((HEADS, 2 * DH, DH), BF16),
+        dma((2,)), dma((2,)),
+        dma((2,)), dma((2,)),
         dma((15,)),
         dma((8,)),
         dma((NX - 1,)), dma((NX - 1,)),

time: 71.5 us -> 72.7 us (1.017)
  the two profiles are of different devices: /device:TPU:312 before, /device:TPU:8 now
where the time goes in v5:
time: 72.7 us; the launch traced here: 72.5 us
  Pallas kernels  71.9 us (99%)
    pallas_call x1, Pallas kernels, shards(): pl.pallas_call(kernel, out_shape=shapes, in_specs=[hbm] * 9, out_specs=(h...  69.8 us
    pallas_call x1, Pallas kernels, shards(): pl.pallas_call(copy_out, out_shape=shapes, in_specs=[hbm] * 8, out_specs=...  2.02 us

profile of v5, /device:TPU:8, one launch (start us, length us, event | category | flops | bytes accessed | tf_op | source)
XLA Modules:
  0.0 72.5 jit_solution(1047783301747592300)
XLA Ops:
  0.6 69.8 %shard_map.152 = (bf16[128,512]{1,0:T(8,128)(2,1)}, bf16[128,512]{1,0:T(8,128)(2,1)}, bf16[128,512]{1,0:T(8,128)(2,1)}, bf16[128,512]{1,0:T(8,128)(2,1)}, bf16[1...) custom-call(bf16[128,512]{1,0:T(8,128)(2,1)} %q_hbm.1, ...), custom_call_target="tpu_custom_call" | custom-call | tf_op jit(solution)/shard_map/pallas_call | solution.py:751
  70.5 2.0 %shard_map.153 = (bf16[128,512]{1,0:T(8,128)(2,1)}, bf16[128,512]{1,0:T(8,128)(2,1)}, bf16[128,512]{1,0:T(8,128)(2,1)}, bf16[128,512]{1,0:T(8,128)(2,1)}, bf16[1...) custom-call(bf16[128,512]{1,0:T(8,128)(2,1)} %get-tuple-element.16.refs_0_, ...), custom_call_target="tpu_custom_call" | custom-call | tf_op jit(solution)/shard_map/pallas_call | solution.py:761

commit v6 on v3

--- a/solution.py
+++ b/solution.py
@@ -127,10 +127,10 @@
             kg.at[y, owner], kg.at[y, owner], kx_s.at[dx - 1], kx_r.at[dx - 1], at(y, col(dx))
         )
 
-    def value_across(row, i, owner):
+    def value_across(row, dx, owner):
         return push(
-            vg.at[row, owner], vg.at[row, owner], vx_s.at[row, i], vx_r.at[row, i],
-            at(y, col(-sigma if i == 1 else sigma)),
+            vg.at[row, owner], vg.at[row, owner], vx_s.at[row, dx - 1], vx_r.at[row, dx - 1],
+            at(y, col(dx)),
         )
 
     def key_ring(place, row, j, turn):
@@ -153,8 +153,8 @@
     for j in (NX, 0):
         key_start(1, y, j, sigma, 4)
         key_start(2, y, j, -sigma, 3)
-    value_across(y, 0, x).start()
-    value_across(y, 1, x).start()
+    for dx in range(1, NX):
+        value_across(y, dx, x).start()
 
     def row_scores(row, masked):
         for b in range(NX):
@@ -239,20 +239,14 @@
     def value_pass(row):
         @when(row < y)
         def _():
-            value_across(row, 0, x).start()
-            value_across(row, 1, x).start()
-
-    def value_relay(row):
-        @when(row <= y)
-        def _():
-            value_across(row, 0, col(-sigma)).wait_recv()
-            value_across(row, 2, col(-sigma)).start()
+            for dx in range(1, NX):
+                value_across(row, dx, x).start()
 
     def value_take(row):
         @when(row <= y)
         def _():
-            value_across(row, 1, col(sigma)).wait_recv()
-            value_across(row, 2, col(2)).wait_recv()
+            for dx in range(1, NX):
+                value_across(row, dx, col(-dx)).wait_recv()
             for b in range(NX):
                 rows = slice(b * ROWS, (b + 1) * ROWS)
                 for cols in halves:
@@ -278,12 +272,6 @@
             return 0
 
         lax.fori_loop(0, NX, block_turn, 0)
-        value_relay(past_a)
-
-        @when(k > 1)
-        def _():
-            value_relay(past_b)
-
         @when(row_a < y)
         def _():
             row_scores(row_a, False)
@@ -315,14 +303,10 @@
         return 0
 
     lax.fori_loop(0, NX, far_turn, 0)
-    value_relay(past_a)
-    value_relay(past_b)
 
     @when(row_far < y)
     def _():
         row_scores(row_far, False)
-
-    value_relay(row_far)
 
     for h in range(NX):
         @when(h != x)
@@ -404,11 +388,10 @@
     def grad_sent(row, turn, sender, far):
         return jnp.where(turn < 0, row < sender, row < far)
 
-    def dv_across(row, i, straight):
-        owner = col((sigma, -sigma, 2)[i])
-        target = owner if i < 2 else jnp.where(straight, owner, col(sigma))
+    def dv_across(row, dx):
         return push(
-            dvp.at[row, owner], vr.at[row, i], du_s.at[row, i], du_r.at[row, i], at(y, target)
+            dvp.at[row, col(dx)], vr.at[row, dx - 1], du_s.at[row, dx - 1], du_r.at[row, dx - 1],
+            at(y, col(dx)),
         )
 
     def dv_ring(place, turn):
@@ -416,19 +399,15 @@
             vsum.at[place], vfin.at[place], dw_s.at[place], dw_r.at[place], at(ring(y + turn), x)
         )
 
-    def dv_relay(row):
-        @when(row <= y)
-        def _():
-            dv_across(row, 2, False).wait_recv()
-            dvp[row, col(sigma)] = (
-                dvp[row, col(sigma)].astype(F32) + vr[row, 2].astype(F32)
-            ).astype(BF16)
-            dv_across(row, 0, False).start()
-
     def dv_sum(row):
-        dv_across(row, 0, False).wait_recv()
-        dv_across(row, 1, False).wait_recv()
-        return dvp[row, x].astype(F32) + vr[row, 0].astype(F32) + vr[row, 1].astype(F32)
+        for dx in range(1, NX):
+            dv_across(row, dx).wait_recv()
+        return (
+            dvp[row, x].astype(F32)
+            + vr[row, 0].astype(F32)
+            + vr[row, 1].astype(F32)
+            + vr[row, 2].astype(F32)
+        )
 
     def place_row(place):
         forth = (lax.rem(place, 2) == 1) | (place == 0)
@@ -475,12 +454,8 @@
                     ds_ref[rows, cols] = grads.astype(BF16)
                 dkf[b] = mm(ds_ref[rows, :], qs[...]) * SCALE
                 dvp[row, b] = mm(wb_ref[rows, :], gs[...]).astype(BF16)
-            dv_across(row, 2, place == NY - 1).start()
-            dv_across(row, 1, False).start()
-
-            @when(place == NY - 1)
-            def _():
-                dv_across(row, 0, False).start()
+            for dx in range(1, NX):
+                dv_across(row, dx).start()
 
         @when(row > y)
         def _():
@@ -513,11 +488,7 @@
 
         @when(place >= 1)
         def _():
-            dv_relay(place_row(place - 1)[2])
-
-        @when(place >= 2)
-        def _():
-            dv_turn(place - 2)
+            dv_turn(place - 1)
 
         @when(place == 2)
         def _():
@@ -546,9 +517,7 @@
         dv_l[:, cols] = (intra[3, :, cols] + fading * mm(kh, later)).astype(BF16)
         return 0
 
-    lax.fori_loop(0, HEADS // 2, light_out, 0)
-    dv_turn(NY - 2)
-    lax.fori_loop(HEADS // 2, HEADS, light_out, 0)
+    lax.fori_loop(0, HEADS, light_out, 0)
     moves = [(o_l, o_hbm), (dq_l, dq_hbm), (dk_l, dk_hbm), (dv_l, dv_hbm)]
     moves += [(o_s, os_hbm), (dq_s, dqs_hbm), (dk_s, dks_hbm), (dv_s, dvs_hbm)]
     stores = [
@@ -591,9 +560,9 @@
     for row in range(NY):
         @when(row <= y)
         def _():
-            for i in range(3):
-                value_across(row, i, x).wait_send()
-                dv_across(row, i, False).wait_send()
+            for dx in range(1, NX):
+                value_across(row, dx, x).wait_send()
+                dv_across(row, dx).wait_send()
 
     def dk_across(dx):
         return push(
@@ -617,8 +586,7 @@
     stores[4].start()
     stores[5].start()
 
-    dv_across(y, 2, True).wait_recv()
-    vacc[...] = dv_sum(y) + vr[y, 2].astype(F32)
+    vacc[...] = dv_sum(y)
     for place, turn, far in ((NY - 3, sigma, 4), (NY - 2, -sigma, 3)):
         @when(grad_sent(y, turn, ring(y - turn), far))
         def _():

time: 71.5 us -> 64.3 us (0.90)
  the two profiles are of different devices: /device:TPU:312 before, /device:TPU:192 now
where the time goes in v6:
time: 64.3 us; the launch traced here: 64.1 us
  Pallas kernels  63.5 us (99%)
    pallas_call x1, Pallas kernels, shards(): pl.pallas_call(kernel, out_shape=shapes, in_specs=[hbm] * 9, out_specs=(h...  61.5 us
    pallas_call x1, Pallas kernels, shards(): pl.pallas_call(copy_out, out_shape=shapes, in_specs=[hbm] * 8, out_specs=...  2.02 us

profile of v6, /device:TPU:192, one launch (start us, length us, event | category | flops | bytes accessed | tf_op | source)
XLA Modules:
  0.0 64.1 jit_solution(7462841506711123458)
XLA Ops:
  0.6 61.5 %shard_map.152 = (bf16[128,512]{1,0:T(8,128)(2,1)}, bf16[128,512]{1,0:T(8,128)(2,1)}, bf16[128,512]{1,0:T(8,128)(2,1)}, bf16[128,512]{1,0:T(8,128)(2,1)}, bf16[1...) custom-call(bf16[128,512]{1,0:T(8,128)(2,1)} %q_hbm.1, ...), custom_call_target="tpu_custom_call" | custom-call | tf_op jit(solution)/shard_map/pallas_call | solution.py:690
  62.1 2.0 %shard_map.153 = (bf16[128,512]{1,0:T(8,128)(2,1)}, bf16[128,512]{1,0:T(8,128)(2,1)}, bf16[128,512]{1,0:T(8,128)(2,1)}, bf16[128,512]{1,0:T(8,128)(2,1)}, bf16[1...) custom-call(bf16[128,512]{1,0:T(8,128)(2,1)} %get-tuple-element.16.refs_0_, ...), custom_call_target="tpu_custom_call" | custom-call | tf_op jit(solution)/shard_map/pallas_call | solution.py:700

commit v7 on v6

--- a/solution.py
+++ b/solution.py
@@ -450,10 +450,10 @@
                 for cols in halves:
                     weights = e_ref[row, rows, cols] * stat_l[pl.ds(row * NX + b, 1), cols]
                     grads = weights * (dp_ref[row, rows, cols] - dot_ref[0:1, cols])
-                    wb_ref[rows, cols] = weights.astype(BF16)
-                    ds_ref[rows, cols] = grads.astype(BF16)
-                dkf[b] = mm(ds_ref[rows, :], qs[...]) * SCALE
-                dvp[row, b] = mm(wb_ref[rows, :], gs[...]).astype(BF16)
+                    wb_ref[row, rows, cols] = weights.astype(BF16)
+                    ds_ref[row, rows, cols] = grads.astype(BF16)
+                dkf[b] = mm(ds_ref[row, rows, :], qs[...]) * SCALE
+                dvp[row, b] = mm(wb_ref[row, rows, :], gs[...]).astype(BF16)
             for dx in range(1, NX):
                 dv_across(row, dx).start()
 
@@ -480,11 +480,6 @@
             return 0
 
         lax.fori_loop(0, NX, ring_block, 0)
-
-        @when(row <= y)
-        def _():
-            out_t[...] += mm_tn(vg[row].reshape(SPAN, DH), wb_ref[...])
-            dq_t[...] += mm_tn(kg[row].reshape(SPAN, DH), ds_ref[...])
 
         @when(place >= 1)
         def _():
@@ -580,6 +575,12 @@
             dks[b] = dkf[b].astype(BF16)
             dk_across(j).start()
 
+    def query_turn(row, _):
+        out_t[...] += mm_tn(vg[row].reshape(SPAN, DH), wb_ref[row])
+        dq_t[...] += mm_tn(kg[row].reshape(SPAN, DH), ds_ref[row])
+        return 0
+
+    lax.fori_loop(0, y + 1, query_turn, 0)
     for part in parts:
         o_s[:, part] = out_t[:, part].T.astype(BF16)
         dq_s[:, part] = (dq_t[:, part].T * SCALE).astype(BF16)
@@ -646,8 +647,8 @@
         pltpu.VMEM((NY * NX, WIDE), F32),
         pltpu.VMEM((NY * NX, WIDE), F32),
         pltpu.VMEM((8, WIDE), F32),
-        pltpu.VMEM((SPAN, WIDE), BF16),
-        pltpu.VMEM((SPAN, WIDE), BF16),
+        pltpu.VMEM((NY, SPAN, WIDE), BF16),
+        pltpu.VMEM((NY, SPAN, WIDE), BF16),
         pltpu.VMEM((DH, WIDE), F32),
         pltpu.VMEM((DH, WIDE), F32),
         pltpu.VMEM((NX, ROWS, DH), F32),

time: 64.3 us -> 64.5 us (level)
  the two profiles are of different devices: /device:TPU:192 before, /device:TPU:8 now
where the time goes in v7:
time: 64.5 us; the launch traced here: 64.3 us
  Pallas kernels  63.6 us (99%)
    pallas_call x1, Pallas kernels, shards(): pl.pallas_call(kernel, out_shape=shapes, in_specs=[hbm] * 9, out_specs=(h...  61.6 us
    pallas_call x1, Pallas kernels, shards(): pl.pallas_call(copy_out, out_shape=shapes, in_specs=[hbm] * 8, out_specs=...  2.02 us

profile of v7, /device:TPU:8, one launch (start us, length us, event | category | flops | bytes accessed | tf_op | source)
XLA Modules:
  0.0 64.3 jit_solution(8107370379000928382)
XLA Ops:
  0.6 61.6 %shard_map.152 = (bf16[128,512]{1,0:T(8,128)(2,1)}, bf16[128,512]{1,0:T(8,128)(2,1)}, bf16[128,512]{1,0:T(8,128)(2,1)}, bf16[128,512]{1,0:T(8,128)(2,1)}, bf16[1...) custom-call(bf16[128,512]{1,0:T(8,128)(2,1)} %q_hbm.1, ...), custom_call_target="tpu_custom_call" | custom-call | tf_op jit(solution)/shard_map/pallas_call | solution.py:691
  62.3 2.0 %shard_map.153 = (bf16[128,512]{1,0:T(8,128)(2,1)}, bf16[128,512]{1,0:T(8,128)(2,1)}, bf16[128,512]{1,0:T(8,128)(2,1)}, bf16[128,512]{1,0:T(8,128)(2,1)}, bf16[1...) custom-call(bf16[128,512]{1,0:T(8,128)(2,1)} %get-tuple-element.16.refs_0_, ...), custom_call_target="tpu_custom_call" | custom-call | tf_op jit(solution)/shard_map/pallas_call | solution.py:701

commit v8 on v7

--- a/solution.py
+++ b/solution.py
@@ -481,9 +481,9 @@
 
         lax.fori_loop(0, NX, ring_block, 0)
 
-        @when(place >= 1)
-        def _():
-            dv_turn(place - 1)
+        @when(place >= 2)
+        def _():
+            dv_turn(place - 2)
 
         @when(place == 2)
         def _():
@@ -492,6 +492,7 @@
         return 0
 
     lax.fori_loop(0, NY, back_turn, 0)
+    dv_turn(NY - 2)
 
     for b in range(NX):
         @when(b != x)

time: 64.5 us -> 63.3 us (0.981)
  the two profiles are of different devices: /device:TPU:8 before, /device:TPU:392 now
where the time goes in v8:
time: 63.3 us; the launch traced here: 63.1 us
  Pallas kernels  62.5 us (99%)
  between operations  0.64 us (1%)
    pallas_call x1, Pallas kernels, shards(): pl.pallas_call(kernel, out_shape=shapes, in_specs=[hbm] * 9, out_specs=(h...  60.5 us
    pallas_call x1, Pallas kernels, shards(): pl.pallas_call(copy_out, out_shape=shapes, in_specs=[hbm] * 8, out_specs=...  2.02 us

profile of v8, /device:TPU:392, one launch (start us, length us, event | category | flops | bytes accessed | tf_op | source)
XLA Modules:
  0.0 63.1 jit_solution(1664636699817151823)
XLA Ops:
  0.6 60.5 %shard_map.152 = (bf16[128,512]{1,0:T(8,128)(2,1)}, bf16[128,512]{1,0:T(8,128)(2,1)}, bf16[128,512]{1,0:T(8,128)(2,1)}, bf16[128,512]{1,0:T(8,128)(2,1)}, bf16[1...) custom-call(bf16[128,512]{1,0:T(8,128)(2,1)} %q_hbm.1, ...), custom_call_target="tpu_custom_call" | custom-call | tf_op jit(solution)/shard_map/pallas_call | solution.py:692
  61.1 2.0 %shard_map.153 = (bf16[128,512]{1,0:T(8,128)(2,1)}, bf16[128,512]{1,0:T(8,128)(2,1)}, bf16[128,512]{1,0:T(8,128)(2,1)}, bf16[128,512]{1,0:T(8,128)(2,1)}, bf16[1...) custom-call(bf16[128,512]{1,0:T(8,128)(2,1)} %get-tuple-element.16.refs_0_, ...), custom_call_target="tpu_custom_call" | custom-call | tf_op jit(solution)/shard_map/pallas_call | solution.py:702
